TPU v7x, 128 devices: a whole 4x4x4 slice. The times are simulated.
128 devices in a mesh: dp: 32 (over z, y, core), feat: 4 (over x).
Axes of the slice: x: 4, y: 4, z: 4, core: 2. Of those that a mesh axis runs over, the one named last changes fastest.
Arguments:
- features: bfloat16 [131072, 8192], P('dp', 'feat'), may hold values from -6 to 6
- fixed_weight: float32 [8192], P('feat'), may hold values from -0.0625 to 0.0625
- prior_offset: float32 [131072], P('dp'), may hold values from -6 to 6
- labels: int32 [131072], P('dp'), may hold values 0 or 1
- impression_member: int32 [131072], P(('dp', 'feat')), may hold values from 0 to 4095, as said below
- member_position: int32 [4096], replicated, may hold values from 0 to 4095, as said below
- member_counts: int32 [4096], P(('dp', 'feat')), may hold values from 0 to 128, as said below
- member_features: float32 [131072, 256], P(('dp', 'feat')), may hold values from -6 to 6
- member_params: float32 [4096, 256], P(('dp', 'feat')), may hold values from -0.375 to 0.375
Outputs:
- updated_weight: float32 [8192], P('feat')
- updated_params: float32 [4096, 256], P(('dp', 'feat'))
- total_margin: float32 [131072], P(('dp', 'feat'))
Inputs may be any that keep to these rules, and one draw needn't show every extreme that they name: `impression_member`: among the 1024 rows of one device, at most 16 name members whose position lies with any one owner (owner = member_position[id] // 32, devices in dp+feat order), and at most 1 names any one member; in every draw one owner receives exactly 16 rows from every device. `member_position`: A permutation of the positions; position p is row p % 32 of device p // 32 of dp+feat. `member_counts`: the number of examples whose member sits at each position.
All inputs are finite; a program needn't handle non-finite values. No bound on the sum of `labels` on one device may be relied on, other than what follows from the above.
Results may differ from a plain program's by a relative error of at most 0.0026.
Values sent between devices are 32-bit elements; how exact they have to be, the bound alone decides.
No kernel may reach another device: no remote copies, remote signals or barrier semaphores. Data moves between devices by JAX's collectives and lax.ppermute only.
A program may use at most 128 MiB of HBM per device.

v0:
```python
import functools

import jax
import jax.numpy as jnp
from jax import lax
from jax.experimental import pallas as pl
from jax.experimental.pallas import tpu as pltpu
from jax.sharding import Mesh
from jax.sharding import PartitionSpec as P

RIDGE_FIXED = 0.1
STEP_FIXED = 2.0
RIDGE_MEMBER = 0.25
TINY = 1e-30
CG_STEPS = 3
F32 = jnp.float32
BF16 = jnp.bfloat16
LANES = 128
CAPACITY = 16
ALL = ("z", "y", "core", "feat")
NN = (((1,), (0,)), ((), ()))
NT = (((1,), (1,)), ((), ()))
TN = (((0,), (0,)), ((), ()))
VMEM_SPEC = pl.BlockSpec(memory_space=pltpu.VMEM)


def dot(left, right, dims):
    return lax.dot_general(left, right, dims, preferred_element_type=F32)


def split(value):
    high = value.astype(BF16)
    return high, (value - high.astype(F32)).astype(BF16)


def dot_split(left, high, low, dims):
    left_high, left_low = split(left)
    rows = left.shape[0]
    both = dot(jnp.concatenate([left_high, left_low], axis=0), high, dims)
    return both[:rows] + both[rows:] + dot(left_high, low, dims)


def sublane_iota(shape):
    return lax.broadcasted_iota(jnp.int32, shape, 0)


def lane_iota(shape):
    return lax.broadcasted_iota(jnp.int32, shape, 1)


def hot_rows(count, index):
    shape = (count, index.shape[1])
    return jnp.where(sublane_iota(shape) == index, 1.0, 0.0).astype(BF16)


def params(vmem_mib):
    return pltpu.CompilerParams(vmem_limit_bytes=vmem_mib << 20)


def route_kernel(ids_ref, table_ref, labels_ref, rows_ref, target_ref, buf_ref, meta_ref, *, mem_dev):
    rows = ids_ref.shape[1]
    ids = ids_ref[...]
    table = table_ref[...]
    owner_table = (table // mem_dev).astype(F32).astype(BF16)
    slot_table = (table % mem_dev).astype(F32).astype(BF16)
    both = jnp.concatenate([owner_table, slot_table], axis=1)
    found = dot(both, hot_rows(table.shape[0], ids // LANES), TN)
    low_hot = sublane_iota((LANES, rows)) == ids % LANES
    owner = jnp.sum(jnp.where(low_hot, found[:LANES], 0.0), axis=0, keepdims=True)
    slot = jnp.sum(jnp.where(low_hot, found[LANES:], 0.0), axis=0, keepdims=True)
    owner_hot = sublane_iota((LANES, rows)) == owner.astype(jnp.int32)
    hot = jnp.where(owner_hot, 1.0, 0.0).astype(BF16)
    earlier = jnp.where(sublane_iota((rows, rows)) < lane_iota((rows, rows)), 1.0, 0.0).astype(BF16)
    before = dot(hot, earlier, NN)
    rank = jnp.sum(jnp.where(owner_hot, before, 0.0), axis=0, keepdims=True).astype(jnp.int32)
    target = owner.astype(jnp.int32) * CAPACITY + rank
    target_ref[...] = target
    slot_hot = jnp.where(owner_hot, slot, 0.0).astype(BF16)
    label_hot = jnp.where(owner_hot, labels_ref[...].astype(F32), 0.0).astype(BF16)
    meta_ref[...] = dot(slot_hot, hot_rows(LANES, rank + 4 * CAPACITY), NT) + dot(
        label_hot, hot_rows(LANES, rank + 5 * CAPACITY), NT
    )
    high, low = split(rows_ref[...])
    parts = jnp.concatenate([high, low], axis=1)
    width = rows_ref.shape[1]
    step = 256
    for start in range(0, buf_ref.shape[0], step):
        place = jnp.where(sublane_iota((step, rows)) + start == target, 1.0, 0.0).astype(BF16)
        moved = dot(place, parts, NN)
        buf_ref[start : start + step, :] = moved[:, :width] + moved[:, width:]


def route(ids, table, labels, rows, mem_dev):
    count = ids.shape[1]
    slots = LANES * CAPACITY
    return pl.pallas_call(
        functools.partial(route_kernel, mem_dev=mem_dev),
        in_specs=[VMEM_SPEC] * 4,
        out_specs=[VMEM_SPEC] * 3,
        out_shape=[
            jax.ShapeDtypeStruct((1, count), jnp.int32),
            jax.ShapeDtypeStruct((slots, rows.shape[1]), F32),
            jax.ShapeDtypeStruct((LANES, LANES), F32),
        ],
        compiler_params=params(32),
        name="route",
    )(ids, table, labels, rows)


def margin_chunk(weight, feat_ref, start, size):
    columns = feat_ref.shape[1]
    half = columns // 2
    matrix = dot(weight[:, :half].astype(BF16), feat_ref[start : start + size, :half], NT)
    sums = []
    sub = 64
    for first in range(start, start + size, sub):
        total = None
        for column in range(half, columns, LANES):
            term = feat_ref[first : first + sub, column : column + LANES].astype(F32) * weight[
                0:1, column : column + LANES
            ]
            total = term if total is None else total + term
        sums.append(total)
    high, low = split(jnp.concatenate(sums, axis=0))
    ones = jnp.ones((8, LANES), BF16)
    return matrix + dot(ones, high, NT) + dot(ones, low, NT)


def margin_kernel(weight_ref, feat_hbm, margin_ref, feat_ref, sems, *, chunks):
    size = feat_ref.shape[0] // chunks
    copies = [
        pltpu.make_async_copy(
            feat_hbm.at[pl.ds(i * size, size)], feat_ref.at[pl.ds(i * size, size)], sems.at[i]
        )
        for i in range(chunks)
    ]
    for copy in copies:
        copy.start()
    weight = jnp.broadcast_to(weight_ref[...].astype(BF16).astype(F32), (8, weight_ref.shape[1]))
    for i in range(chunks):
        copies[i].wait()
        margin_ref[:, i * size : (i + 1) * size] = margin_chunk(weight, feat_ref, i * size, size)[0:1]


def margin_pass(weight, features):
    rows, columns = features.shape
    chunks = 8
    return pl.pallas_call(
        functools.partial(margin_kernel, chunks=chunks),
        in_specs=[VMEM_SPEC, pl.BlockSpec(memory_space=pl.ANY)],
        out_specs=[VMEM_SPEC, VMEM_SPEC],
        out_shape=[jax.ShapeDtypeStruct((1, rows), F32), pltpu.VMEM((rows, columns), BF16)],
        scratch_shapes=[pltpu.SemaphoreType.DMA((chunks,))],
        compiler_params=params(24),
        name="margin",
    )(weight, features)


def grad_kernel(m0, m1, m2, m3, offset_ref, labels_ref, feat_ref, grad_ref):
    margin = (m0[...] + m2[...]) + (m1[...] + m3[...]) + offset_ref[...]
    residual = (jax.nn.sigmoid(margin) - labels_ref[...].astype(F32)).astype(BF16)
    grad_ref[...] = dot(jnp.broadcast_to(residual, (8, residual.shape[1])), feat_ref[...], NN)[0:1]


def grad_pass(margins, offset, labels, features):
    columns = features.shape[1]
    return pl.pallas_call(
        grad_kernel,
        in_specs=[VMEM_SPEC] * 7,
        out_specs=VMEM_SPEC,
        out_shape=jax.ShapeDtypeStruct((1, columns), F32),
        compiler_params=params(24),
        name="grad",
    )(*margins, offset, labels, pltpu.with_memory_space_constraint(features, pltpu.VMEM))


def new_kernel(
    me_ref, g0, g1, g2, g3, weight_ref, meta_ref, t0, t1, t2, t3, feat_ref, updated_ref, send_ref, *, examples
):
    gradient = ((g0[...] + g2[...]) + (g1[...] + g3[...])) / examples + RIDGE_FIXED * weight_ref[...]
    updated = weight_ref[...] - STEP_FIXED * gradient
    updated_ref[...] = updated
    weight = jnp.broadcast_to(updated.astype(BF16).astype(F32), (8, updated.shape[1]))
    mine = me_ref[0]
    block = t0.shape[1]
    send = meta_ref[...]
    for hop, target_ref in enumerate((t0, t1, t2, t3)):
        number = lax.rem(mine - hop + 4, 4)
        pieces = []
        size = 256
        first = pl.multiple_of(number * block, block)
        for start in range(0, block, size):
            pieces.append(margin_chunk(weight, feat_ref.at[pl.ds(first + start, size)], 0, size)[0:1])
        scores = jnp.concatenate(pieces, axis=1)
        target = target_ref[...]
        owner = target // CAPACITY
        lane = number * CAPACITY + target % CAPACITY
        owner_hot = sublane_iota((LANES, block)) == owner
        spread = jnp.where(owner_hot, scores, 0.0)
        high, low = split(spread)
        lane_hot = hot_rows(LANES, lane)
        both = dot(jnp.concatenate([high, low], axis=0), lane_hot, NT)
        send = send + both[:LANES] + both[LANES:]
    send_ref[...] = send


def new_pass(me, grads, weight, meta, targets, features, examples):
    columns = features.shape[1]
    return pl.pallas_call(
        functools.partial(new_kernel, examples=examples),
        in_specs=[pl.BlockSpec(memory_space=pltpu.SMEM)] + [VMEM_SPEC] * 11,
        out_specs=[VMEM_SPEC] * 2,
        out_shape=[
            jax.ShapeDtypeStruct((1, columns), F32),
            jax.ShapeDtypeStruct((LANES, LANES), F32),
        ],
        compiler_params=params(24),
        name="new",
    )(me, *grads, weight, meta, *targets, pltpu.with_memory_space_constraint(features, pltpu.VMEM))


def prepare_kernel(rows_ref, params_ref, high_ref, low_ref, score_ref):
    high, low = split(rows_ref[...])
    high_ref[...] = high
    low_ref[...] = low
    score_ref[...] = dot_split(params_ref[...], high, low, NT)


def prepare(rows, member_params):
    slots, width = rows.shape
    members = member_params.shape[0]
    return pl.pallas_call(
        prepare_kernel,
        in_specs=[VMEM_SPEC] * 2,
        out_specs=[VMEM_SPEC] * 3,
        out_shape=[
            jax.ShapeDtypeStruct((slots, width), BF16),
            jax.ShapeDtypeStruct((slots, width), BF16),
            jax.ShapeDtypeStruct((members, slots), F32),
        ],
        compiler_params=params(24),
        name="prepare",
    )(rows, member_params)


def to_row(table):
    return jnp.concatenate([table[i : i + 1, :] for i in range(table.shape[0])], axis=1)


def members_kernel(recv_ref, high_ref, low_ref, score_ref, params_ref, counts_ref, out_ref, back_ref):
    tiles = high_ref.shape[0] // LANES
    lane = lane_iota((tiles, LANES))
    even = jnp.zeros((tiles, LANES), F32)
    odd = jnp.zeros((tiles, LANES), F32)
    slots = jnp.zeros((tiles, LANES), F32)
    labels = jnp.zeros((tiles, LANES), F32)
    for q in range(8):
        piece = recv_ref[pl.ds(q, tiles, stride=8), :]
        if q < 4:
            even += piece
        else:
            odd += piece
        here = lane // CAPACITY == q
        slots = jnp.where(here, pltpu.roll(piece, (q * CAPACITY - 4 * CAPACITY) % LANES, 1), slots)
        labels = jnp.where(here, pltpu.roll(piece, (q * CAPACITY - 5 * CAPACITY) % LANES, 1), labels)
    offset = to_row(jnp.where(lane < LANES // 2, even, pltpu.roll(odd, LANES // 2, 1)))
    slot = to_row(slots).astype(jnp.int32)
    label = to_row(labels)
    members = params_ref.shape[0]
    mask = sublane_iota((members, slot.shape[1])) == slot

    def own(value):
        return jnp.sum(jnp.where(mask, value, 0.0), axis=0, keepdims=True)

    high, low = high_ref[...], low_ref[...]
    old = params_ref[...]
    scaling = 1.0 / (counts_ref[...].astype(F32) + 1.0)
    margin = offset + own(score_ref[...])
    probability = jax.nn.sigmoid(margin)
    weight = probability * (1.0 - probability)
    errors = jnp.where(mask, label - probability, 0.0)
    remains = scaling * dot_split(errors, high, low, NN) - RIDGE_MEMBER * old
    direction = remains
    delta = jnp.zeros_like(remains)
    norm_now = jnp.sum(remains * remains, axis=1, keepdims=True)
    for step in range(CG_STEPS):
        along = jnp.where(mask, dot_split(direction, high, low, NT), 0.0)
        weighted = along * weight
        curve = scaling * jnp.sum(weighted * along, axis=1, keepdims=True) + RIDGE_MEMBER * jnp.sum(
            direction * direction, axis=1, keepdims=True
        )
        step_size = norm_now / (curve + TINY)
        delta = delta + step_size * direction
        margin = margin + jnp.sum(along * step_size, axis=0, keepdims=True)
        if step < CG_STEPS - 1:
            image = scaling * dot_split(weighted, high, low, NN) + RIDGE_MEMBER * direction
            remains = remains - step_size * image
            norm_next = jnp.sum(remains * remains, axis=1, keepdims=True)
            direction = remains + (norm_next / (norm_now + TINY)) * direction
            norm_now = norm_next
    out_ref[...] = old + delta
    for t in range(tiles):
        back_ref[8 * t : 8 * t + 8, :] = jnp.broadcast_to(
            margin[:, t * LANES : (t + 1) * LANES], (8, LANES)
        )


def members_pass(recv, high, low, score, member_params, counts):
    return pl.pallas_call(
        members_kernel,
        in_specs=[VMEM_SPEC] * 6,
        out_specs=[VMEM_SPEC] * 2,
        out_shape=[
            jax.ShapeDtypeStruct(member_params.shape, F32),
            jax.ShapeDtypeStruct((LANES, LANES), F32),
        ],
        compiler_params=params(32),
        name="members",
    )(recv, high, low, score, member_params, counts)


def collect_kernel(me_ref, back_ref, target_ref, out_ref):
    target = target_ref[...]
    high, low = split(back_ref[...])
    hot = hot_rows(LANES, target // CAPACITY)
    found = dot(high, hot, TN) + dot(low, hot, TN)
    lane = lax.rem(me_ref[0], 8) * CAPACITY + target % CAPACITY
    here = sublane_iota(found.shape) == lane
    out_ref[...] = jnp.sum(jnp.where(here, found, 0.0), axis=0, keepdims=True)


def collect(me, back, target):
    return pl.pallas_call(
        collect_kernel,
        in_specs=[pl.BlockSpec(memory_space=pltpu.SMEM)] + [VMEM_SPEC] * 2,
        out_specs=VMEM_SPEC,
        out_shape=jax.ShapeDtypeStruct(target.shape, F32),
        compiler_params=params(16),
        name="collect",
    )(me, back, target)


def behind(value, axis):
    size = lax.axis_size(axis)
    return [value] + [
        lax.ppermute(value, axis, [(i, (i + hop) % size) for i in range(size)])
        for hop in range(1, size)
    ]


def other_core(value):
    return lax.ppermute(value, "core", [(0, 1), (1, 0)])


def exchange(table):
    sent = table.reshape(LANES, 1, LANES)
    return lax.all_to_all(sent, ALL, split_axis=0, concat_axis=0, tiled=True).reshape(LANES, LANES)


def body(
    features,
    fixed_weight,
    prior_offset,
    labels,
    impression_member,
    member_position,
    member_counts,
    member_features,
    member_params,
):
    owners = lax.axis_size(ALL)
    mem_dev, width = member_params.shape
    rows = member_features.shape[0]
    examples = features.shape[0] * owners // lax.axis_size("feat")
    place = lax.axis_index("feat")
    me = lax.axis_index(ALL).astype(jnp.int32).reshape(1)
    feat_me = place.astype(jnp.int32).reshape(1)
    weight = fixed_weight[None]
    label_row = labels[None]
    my_labels = lax.dynamic_slice_in_dim(label_row, place * rows, rows, axis=1)

    target, row_buf, meta = route(
        impression_member[None], member_position.reshape(-1, LANES), my_labels, member_features, mem_dev
    )
    got = lax.all_to_all(
        row_buf.reshape(owners, CAPACITY, width), ALL, split_axis=0, concat_axis=0, tiled=True
    ).reshape(owners * CAPACITY, width)
    targets = behind(target, "feat")

    margin, held = margin_pass(weight, features)
    margins = behind(margin, "feat")
    grad = grad_pass(margins, prior_offset[None], label_row, held)
    grad = grad + other_core(grad)
    a, b, c, d = behind(grad, "y")
    grads = behind((a + c) + (b + d), "z")
    updated, send = new_pass(feat_me, grads, weight, meta, targets, held, examples)

    recv = exchange(send)
    high, low, score = prepare(got, member_params)
    updated_params, back = members_pass(recv, high, low, score, member_params, member_counts[:, None])
    total = collect(me, exchange(back), target)
    return updated[0], updated_params, total[0]


def solution(mesh):
    split_mesh = Mesh(mesh.devices.reshape(4, 4, 2, 4), ALL)
    dp = ("z", "y", "core")
    placed = (
        P(dp, "feat"),
        P("feat"),
        P(dp),
        P(dp),
        P(ALL),
        P(),
        P(ALL),
        P(ALL, None),
        P(ALL, None),
    )
    return jax.shard_map(
        body,
        mesh=split_mesh,
        in_specs=placed,
        out_specs=(P("feat"), P(ALL, None), P(ALL)),
        check_vma=False,
    )
```

profile of v0, /device:TPU:1, one launch (start us, length us, event | category | flops | bytes accessed | tf_op | source)
XLA Modules:
  0.0 112.9 jit_solution(10855293609045034388)
XLA Ops:
  0.6 0.7 dynamic-slice.3
  1.4 1.2 %copy-done.3 = f32[1024,256]{1,0:T(8,128)S(1)} copy-done((f32[1024,256]{1,0:T(8,128)S(1)}, f32[1024,256]{1,0:T(8,128)}, u32[]{:S(2)}) %copy-start.3) | copy-done | bytes 1048600
  2.6 0.7 copy-done.8
  3.3 0.7 copy-done.10
  4.0 3.2 %route.1 = (s32[1,1024]{1,0:T(1,128)S(1)}, f32[2048,256]{1,0:T(8,128)S(1)}, f32[128,128]{1,0:T(8,128)S(1)}) custom-call(s32[1,1024]{1,0:T(1,128)S(1)} %bitcast.31, s32[32,128]{1,0:T(8,128)S(1)} %bitcast.28, s32[1,1024]{1,0:T(1,128)S(1)} %bitcast.29, f32[1024,256]{1,0:T(8,128)S(1)} %copy-done.3), custom_call_target="tpu_custom_call" | custom-call | tf_op jit(solution)/shard_map/route/pallas_call | solution.py:96
  7.2 1.3 %copy-done = f32[2048,256]{1,0:T(8,128)} copy-done((f32[2048,256]{1,0:T(8,128)}, f32[2048,256]{1,0:T(8,128)S(1)}, u32[]{:S(2)}) %copy-start) | copy-done | bytes 2097176
  8.6 11.5 %all-to-all-start.1 = ((f32[128,16,256]{2,1,0:T(8,128)}), f32[128,16,256]{2,1,0:T(8,128)S(1)}, u32[]{:S(2)}, u32[]{:S(2)}) async-start(f32[128,16,256]{2,1,0:T(8,128)} %bitcast.22), calls=%async_computation.1 | async-start | bytes 4194304 | tf_op jit(solution)/shard_map/all_to_all | solution.py:385
  20.1 0.0 copy-start.5
  20.1 0.7 copy-done.5
  20.8 6.8 %margin.1 = (f32[1,4096]{1,0:T(1,128)S(1)}, bf16[4096,2048]{1,0:T(8,128)(2,1)S(1)}) custom-call(f32[1,2048]{1,0:T(1,128)S(1)} %bitcast.25, bf16[4096,2048]{1,0:T(8,128)(2,1)} %feat_hbm.1), custom_call_target="tpu_custom_call" | custom-call | tf_op jit(solution)/shard_map/margin/pallas_call | solution.py:148
  27.6 1.5 %collective-permute-start = (f32[1,4096]{1,0:T(1,128)S(1)}, f32[1,4096]{1,0:T(1,128)S(1)}, u32[]{:S(2)}, u32[]{:S(2)}) collective-permute-start(f32[1,4096]{1,0:T(1,128)S(1)} %get-tuple-element.15.m0), channel_id=1, source_target_pairs={{0,1},{1,2},{2,3},{3,0},{4,5},{5,6},{6,7},{7,4},{8,9},{9,10},{10,1... | collective-permute-start | bytes 49160 | tf_op jit(solution)/shard_map/ppermute | solution.py:346
  29.0 2.4 %collective-permute-start.1 = (f32[1,4096]{1,0:T(1,128)S(1)}, f32[1,4096]{1,0:T(1,128)S(1)}, u32[]{:S(2)}, u32[]{:S(2)}) collective-permute-start(f32[1,4096]{1,0:T(1,128)S(1)} %get-tuple-element.15.m0), channel_id=1, source_target_pairs={{0,2},{1,3},{2,0},{3,1},{4,6},{5,7},{6,4},{7,5},{8,10},{9,11},{10,... | collective-permute-start | bytes 49160 | tf_op jit(solution)/shard_map/ppermute | solution.py:346
  31.4 1.2 %collective-permute-start.2 = (f32[1,4096]{1,0:T(1,128)S(1)}, f32[1,4096]{1,0:T(1,128)S(1)}, u32[]{:S(2)}, u32[]{:S(2)}) collective-permute-start(f32[1,4096]{1,0:T(1,128)S(1)} %get-tuple-element.15.m0), channel_id=1, source_target_pairs={{0,3},{1,0},{2,1},{3,2},{4,7},{5,4},{6,5},{7,6},{8,11},{9,8},{10,9... | collective-permute-start | bytes 49160 | tf_op jit(solution)/shard_map/ppermute | solution.py:346
  32.6 12.1 %collective-permute-done.m1 = f32[1,4096]{1,0:T(1,128)S(1)} collective-permute-done((f32[1,4096]{1,0:T(1,128)S(1)}, f32[1,4096]{1,0:T(1,128)S(1)}, u32[]{:S(2)}, u32[]{:S(2)}) %collective-permute-start) | collective-permute-done | bytes 16416 | tf_op jit(solution)/shard_map/ppermute | solution.py:346
  44.7 1.5 %collective-permute-done.1.m2 = f32[1,4096]{1,0:T(1,128)S(1)} collective-permute-done((f32[1,4096]{1,0:T(1,128)S(1)}, f32[1,4096]{1,0:T(1,128)S(1)}, u32[]{:S(2)}, u32[]{:S(2)}) %collective-permute-start.1) | collective-permute-done | bytes 16416 | tf_op jit(solution)/shard_map/ppermute | solution.py:346
  46.3 0.0 collective-permute-done.2.m3
  46.3 0.0 copy-start.11
  46.3 0.0 copy-start.4
  46.3 2.3 %grad.1 = f32[1,2048]{1,0:T(1,128)S(1)} custom-call(f32[1,4096]{1,0:T(1,128)S(1)} %get-tuple-element.15.m0, f32[1,4096]{1,0:T(1,128)S(1)} %collective-permute-done.m1, f32[1,4096]{1,0:T(1,128)S(1)} %collective-permute-done.1.m2, f32[1,4096]{1,0:T(1,128)S(1)} %collective-permute-done.2.m3, f32[1,4096]{1,0:T(1,128)S(1)} %bitcast.30, s32[1,4096]{1,0:T(1,128)S(1)} %bitcast.27, ...), custom_call_target="tpu_custom_call" | custom-call | tf_op jit(solution)/shard_map/grad/pallas_call | solution.py:167
  48.6 0.9 collective-permute-start.3
  49.4 0.8 collective-permute-done.3
  50.3 2.8 %collective-permute-start.4 = (f32[1,2048]{1,0:T(1,128)S(1)}, f32[1,2048]{1,0:T(1,128)S(1)}, u32[]{:S(2)}, u32[]{:S(2)}) collective-permute-start(f32[1,2048]{1,0:T(1,128)S(1)} %add.24), channel_id=1, source_target_pairs={{0,16},{8,24},{16,0},{24,8},{1,17},{9,25},{17,1},{25,9},{2,18},{10... | collective-permute-start | bytes 24584 | tf_op jit(solution)/shard_map/ppermute | solution.py:346
  53.1 0.4 collective-permute-start.5
  53.4 2.3 %collective-permute-start.6 = (f32[1,2048]{1,0:T(1,128)S(1)}, f32[1,2048]{1,0:T(1,128)S(1)}, u32[]{:S(2)}, u32[]{:S(2)}) collective-permute-start(f32[1,2048]{1,0:T(1,128)S(1)} %add.24), channel_id=1, source_target_pairs={{0,24},{8,0},{16,8},{24,16},{1,25},{9,1},{17,9},{25,17},{2,26},{10... | collective-permute-start | bytes 24584 | tf_op jit(solution)/shard_map/ppermute | solution.py:346
  55.8 0.1 collective-permute-start.10
  55.9 0.0 collective-permute-done.4
  55.9 0.9 collective-permute-done.5
  56.8 1.7 %collective-permute-start.7 = (f32[1,2048]{1,0:T(1,128)S(1)}, f32[1,2048]{1,0:T(1,128)S(1)}, u32[]{:S(2)}, u32[]{:S(2)}) collective-permute-start(f32[1,2048]{1,0:T(1,128)S(1)} %add_add_fusion.g0), channel_id=1, source_target_pairs={{0,32},{32,64},{64,96},{96,0},{1,33},{33,65},{65,97},{97,1},{2,34}... | collective-permute-start | bytes 24584 | tf_op jit(solution)/shard_map/ppermute | solution.py:346
  58.5 2.9 %collective-permute-start.8 = (f32[1,2048]{1,0:T(1,128)S(1)}, f32[1,2048]{1,0:T(1,128)S(1)}, u32[]{:S(2)}, u32[]{:S(2)}) collective-permute-start(f32[1,2048]{1,0:T(1,128)S(1)} %add_add_fusion.g0), channel_id=1, source_target_pairs={{0,64},{32,96},{64,0},{96,32},{1,65},{33,97},{65,1},{97,33},{2,66}... | collective-permute-start | bytes 24584 | tf_op jit(solution)/shard_map/ppermute | solution.py:346
  61.4 0.9 collective-permute-start.9
  62.4 0.9 collective-permute-start.11
  63.2 0.0 collective-permute-done.10.t1
  63.2 1.6 %collective-permute-start.12 = (s32[1,1024]{1,0:T(1,128)S(1)}, s32[1,1024]{1,0:T(1,128)S(1)}, u32[]{:S(2)}, u32[]{:S(2)}) collective-permute-start(s32[1,1024]{1,0:T(1,128)S(1)} %get-tuple-element.18.t0.target_ref), channel_id=1, source_target_pairs={{0,3},{1,0},{2,1},{3,2},{4,7},{5,4},{6,5},{7,6},{8,11},{9,8},{10,9... | collective-permute-start | bytes 12296 | tf_op jit(solution)/shard_map/ppermute | solution.py:346
  64.9 1.4 %collective-permute-done.11.t2 = s32[1,1024]{1,0:T(1,128)S(1)} collective-permute-done((s32[1,1024]{1,0:T(1,128)S(1)}, s32[1,1024]{1,0:T(1,128)S(1)}, u32[]{:S(2)}, u32[]{:S(2)}) %collective-permute-start.11) | collective-permute-done | bytes 4128 | tf_op jit(solution)/shard_map/ppermute | solution.py:346
  66.3 0.0 collective-permute-done.12.t3
  66.3 0.0 collective-permute-done.7.g1
  66.4 4.9 %new.1 = (f32[1,2048]{1,0:T(1,128)}, f32[128,128]{1,0:T(8,128)}) custom-call(s32[1]{0:T(128)} %bitcast.me_ref, f32[1,2048]{1,0:T(1,128)S(1)} %add_add_fusion.g0, f32[1,2048]{1,0:T(1,128)S(1)} %collective-permute-done.7.g1, f32[1,2048]{1,0:T(1,128)S(1)} %collective-permute-done.8.g2, f32[1,2048]{1,0:T(1,128)S(1)} %collective-permute-done.9.g3, ...), custom_call_target="tpu_custom_call" | custom-call | tf_op jit(solution)/shard_map/new/pallas_call | solution.py:209
  71.2 10.3 %all-to-all-start = ((f32[128,1,128]{2,1,0:T(1,128)}), f32[128,1,128]{2,1,0:T(1,128)S(1)}, u32[]{:S(2)}, u32[]{:S(2)}) async-start(f32[128,1,128]{2,1,0:T(1,128)} %bitcast.9), calls=%async_computation | async-start | bytes 131072 | tf_op jit(solution)/shard_map/all_to_all | solution.py:357
  81.6 0.1 copy.14.counts_ref
  81.7 0.8 prepare.1
  82.4 0.0 copy-start.1
  82.5 1.0 copy-done.1
  83.4 7.8 %all-to-all-done = f32[128,1,128]{2,1,0:T(1,128)S(1)} async-done(((f32[128,1,128]{2,1,0:T(1,128)}), f32[128,1,128]{2,1,0:T(1,128)S(1)}, u32[]{:S(2)}, u32[]{:S(2)}) %all-to-all-start) | async-done | bytes 65568 | tf_op jit(solution)/shard_map/all_to_all | solution.py:357
  91.3 1.2 %copy-done.2 = bf16[2048,256]{1,0:T(8,128)(2,1)S(1)} copy-done((bf16[2048,256]{1,0:T(8,128)(2,1)S(1)}, bf16[2048,256]{1,0:T(8,128)(2,1)}, u32[]{:S(2)}) %copy-start.2) | copy-done | bytes 1048600
  92.5 5.5 %members.1 = (f32[32,256]{1,0:T(8,128)}, f32[128,128]{1,0:T(8,128)}) custom-call(f32[128,128]{1,0:T(8,128)S(1)} %bitcast.23, bf16[2048,256]{1,0:T(8,128)(2,1)S(1)} %get-tuple-element.22.high_ref, bf16[2048,256]{1,0:T(8,128)(2,1)S(1)} %copy-done.2, f32[32,2048]{1,0:T(8,128)S(1)} %get-tuple-element.24.score_ref, f32[32,256]{1,0:T(8,128)S(1)} %copy-done.4, ...), custom_call_target="tpu_custom_call" | custom-call | tf_op jit(solution)/shard_map/members/pallas_call | solution.py:309
  98.0 4.3 %all-to-all-start.2 = ((f32[128,1,128]{2,1,0:T(1,128)}), f32[128,1,128]{2,1,0:T(1,128)S(1)}, u32[]{:S(2)}, u32[]{:S(2)}) async-start(f32[128,1,128]{2,1,0:T(1,128)} %bitcast.16), calls=%async_computation.2 | async-start | bytes 131072 | tf_op jit(solution)/shard_map/all_to_all | solution.py:357
  102.3 9.7 %all-to-all-done.2 = f32[128,1,128]{2,1,0:T(1,128)S(1)} async-done(((f32[128,1,128]{2,1,0:T(1,128)}), f32[128,1,128]{2,1,0:T(1,128)S(1)}, u32[]{:S(2)}, u32[]{:S(2)}) %all-to-all-start.2) | async-done | bytes 65568 | tf_op jit(solution)/shard_map/all_to_all | solution.py:357
  111.9 0.9 collect.1
  (19 shorter events, 0.1 us)
Async XLA Ops:
  0.6 45.6 %copy-start.7 = (s32[4096]{0:T(1024)S(1)}, s32[4096]{0:T(1024)}, u32[]{:S(2)}) copy-start(s32[4096]{0:T(1024)} %param.12) | copy-start | bytes 49156
  1.4 1.2 %copy-start.3 = (f32[1024,256]{1,0:T(8,128)S(1)}, f32[1024,256]{1,0:T(8,128)}, u32[]{:S(2)}) copy-start(f32[1024,256]{1,0:T(8,128)} %rows_ref.1) | copy-start | bytes 3145732
  2.6 0.7 copy-start.8
  3.3 0.7 copy-start.10
  4.0 42.2 %copy-start.9 = (f32[4096]{0:T(1024)S(1)}, f32[4096]{0:T(1024)}, u32[]{:S(2)}) copy-start(f32[4096]{0:T(1024)} %param.11) | copy-start | bytes 49156
  7.2 1.3 %copy-start = (f32[2048,256]{1,0:T(8,128)}, f32[2048,256]{1,0:T(8,128)S(1)}, u32[]{:S(2)}) copy-start(f32[2048,256]{1,0:T(8,128)S(1)} %get-tuple-element.21) | copy-start | bytes 6291460
  8.6 62.6 %all-to-all-start.1 = ((f32[128,16,256]{2,1,0:T(8,128)}), f32[128,16,256]{2,1,0:T(8,128)S(1)}, u32[]{:S(2)}, u32[]{:S(2)}) async-start(f32[128,16,256]{2,1,0:T(8,128)} %bitcast.22), calls=%async_computation.1 | async-start | bytes 4194304 | tf_op jit(solution)/shard_map/all_to_all | solution.py:385
  20.1 0.7 copy-start.5
  20.8 45.6 %copy-start.6 = (f32[2048]{0:T(1024)S(1)}, f32[2048]{0:T(1024)}, u32[]{:S(2)}) copy-start(f32[2048]{0:T(1024)} %param.10) | copy-start | bytes 24580
  27.6 17.2 %collective-permute-start = (f32[1,4096]{1,0:T(1,128)S(1)}, f32[1,4096]{1,0:T(1,128)S(1)}, u32[]{:S(2)}, u32[]{:S(2)}) collective-permute-start(f32[1,4096]{1,0:T(1,128)S(1)} %get-tuple-element.15.m0), channel_id=1, source_target_pairs={{0,1},{1,2},{2,3},{3,0},{4,5},{5,6},{6,7},{7,4},{8,9},{9,10},{10,1... | collective-permute-start | bytes 49160 | tf_op jit(solution)/shard_map/ppermute | solution.py:346
  29.0 17.2 %collective-permute-start.1 = (f32[1,4096]{1,0:T(1,128)S(1)}, f32[1,4096]{1,0:T(1,128)S(1)}, u32[]{:S(2)}, u32[]{:S(2)}) collective-permute-start(f32[1,4096]{1,0:T(1,128)S(1)} %get-tuple-element.15.m0), channel_id=1, source_target_pairs={{0,2},{1,3},{2,0},{3,1},{4,6},{5,7},{6,4},{7,5},{8,10},{9,11},{10,... | collective-permute-start | bytes 49160 | tf_op jit(solution)/shard_map/ppermute | solution.py:346
  31.4 14.8 %collective-permute-start.2 = (f32[1,4096]{1,0:T(1,128)S(1)}, f32[1,4096]{1,0:T(1,128)S(1)}, u32[]{:S(2)}, u32[]{:S(2)}) collective-permute-start(f32[1,4096]{1,0:T(1,128)S(1)} %get-tuple-element.15.m0), channel_id=1, source_target_pairs={{0,3},{1,0},{2,1},{3,2},{4,7},{5,4},{6,5},{7,6},{8,11},{9,8},{10,9... | collective-permute-start | bytes 49160 | tf_op jit(solution)/shard_map/ppermute | solution.py:346
  46.3 35.3 %copy-start.11 = (s32[32]{0:T(128)S(1)}, s32[32]{0:T(128)}, u32[]{:S(2)}) copy-start(s32[32]{0:T(128)} %param.15) | copy-start | bytes 388
  46.3 35.4 %copy-start.4 = (f32[32,256]{1,0:T(8,128)S(1)}, f32[32,256]{1,0:T(8,128)}, u32[]{:S(2)}) copy-start(f32[32,256]{1,0:T(8,128)} %params_ref.3) | copy-start | bytes 98308
  48.6 1.7 %collective-permute-start.3 = (f32[1,2048]{1,0:T(1,128)S(1)}, f32[1,2048]{1,0:T(1,128)S(1)}, u32[]{:S(2)}, u32[]{:S(2)}) collective-permute-start(f32[1,2048]{1,0:T(1,128)S(1)} %grad.1), channel_id=1, source_target_pairs={{0,4},{4,0},{1,5},{5,1},{2,6},{6,2},{3,7},{7,3},{8,12},{12,8},{9,1... | collective-permute-start | bytes 24584 | tf_op jit(solution)/shard_map/ppermute | solution.py:352
  50.3 5.6 %collective-permute-start.4 = (f32[1,2048]{1,0:T(1,128)S(1)}, f32[1,2048]{1,0:T(1,128)S(1)}, u32[]{:S(2)}, u32[]{:S(2)}) collective-permute-start(f32[1,2048]{1,0:T(1,128)S(1)} %add.24), channel_id=1, source_target_pairs={{0,16},{8,24},{16,0},{24,8},{1,17},{9,25},{17,1},{25,9},{2,18},{10... | collective-permute-start | bytes 24584 | tf_op jit(solution)/shard_map/ppermute | solution.py:346
  53.1 3.7 %collective-permute-start.5 = (f32[1,2048]{1,0:T(1,128)S(1)}, f32[1,2048]{1,0:T(1,128)S(1)}, u32[]{:S(2)}, u32[]{:S(2)}) collective-permute-start(f32[1,2048]{1,0:T(1,128)S(1)} %add.24), channel_id=1, source_target_pairs={{0,8},{8,16},{16,24},{24,0},{1,9},{9,17},{17,25},{25,1},{2,10},{10... | collective-permute-start | bytes 24584 | tf_op jit(solution)/shard_map/ppermute | solution.py:346
  53.4 3.4 %collective-permute-start.6 = (f32[1,2048]{1,0:T(1,128)S(1)}, f32[1,2048]{1,0:T(1,128)S(1)}, u32[]{:S(2)}, u32[]{:S(2)}) collective-permute-start(f32[1,2048]{1,0:T(1,128)S(1)} %add.24), channel_id=1, source_target_pairs={{0,24},{8,0},{16,8},{24,16},{1,25},{9,1},{17,9},{25,17},{2,26},{10... | collective-permute-start | bytes 24584 | tf_op jit(solution)/shard_map/ppermute | solution.py:346
  55.8 7.5 %collective-permute-start.10 = (s32[1,1024]{1,0:T(1,128)S(1)}, s32[1,1024]{1,0:T(1,128)S(1)}, u32[]{:S(2)}, u32[]{:S(2)}) collective-permute-start(s32[1,1024]{1,0:T(1,128)S(1)} %get-tuple-element.18.t0.target_ref), channel_id=1, source_target_pairs={{0,1},{1,2},{2,3},{3,0},{4,5},{5,6},{6,7},{7,4},{8,9},{9,10},{10,1... | collective-permute-start | bytes 12296 | tf_op jit(solution)/shard_map/ppermute | solution.py:346
  56.8 9.5 %collective-permute-start.7 = (f32[1,2048]{1,0:T(1,128)S(1)}, f32[1,2048]{1,0:T(1,128)S(1)}, u32[]{:S(2)}, u32[]{:S(2)}) collective-permute-start(f32[1,2048]{1,0:T(1,128)S(1)} %add_add_fusion.g0), channel_id=1, source_target_pairs={{0,32},{32,64},{64,96},{96,0},{1,33},{33,65},{65,97},{97,1},{2,34}... | collective-permute-start | bytes 24584 | tf_op jit(solution)/shard_map/ppermute | solution.py:346
  58.5 7.8 %collective-permute-start.8 = (f32[1,2048]{1,0:T(1,128)S(1)}, f32[1,2048]{1,0:T(1,128)S(1)}, u32[]{:S(2)}, u32[]{:S(2)}) collective-permute-start(f32[1,2048]{1,0:T(1,128)S(1)} %add_add_fusion.g0), channel_id=1, source_target_pairs={{0,64},{32,96},{64,0},{96,32},{1,65},{33,97},{65,1},{97,33},{2,66}... | collective-permute-start | bytes 24584 | tf_op jit(solution)/shard_map/ppermute | solution.py:346
  61.4 4.9 %collective-permute-start.9 = (f32[1,2048]{1,0:T(1,128)S(1)}, f32[1,2048]{1,0:T(1,128)S(1)}, u32[]{:S(2)}, u32[]{:S(2)}) collective-permute-start(f32[1,2048]{1,0:T(1,128)S(1)} %add_add_fusion.g0), channel_id=1, source_target_pairs={{0,96},{32,0},{64,32},{96,64},{1,97},{33,1},{65,33},{97,65},{2,98}... | collective-permute-start | bytes 24584 | tf_op jit(solution)/shard_map/ppermute | solution.py:346
  62.4 4.0 %collective-permute-start.11 = (s32[1,1024]{1,0:T(1,128)S(1)}, s32[1,1024]{1,0:T(1,128)S(1)}, u32[]{:S(2)}, u32[]{:S(2)}) collective-permute-start(s32[1,1024]{1,0:T(1,128)S(1)} %get-tuple-element.18.t0.target_ref), channel_id=1, source_target_pairs={{0,2},{1,3},{2,0},{3,1},{4,6},{5,7},{6,4},{7,5},{8,10},{9,11},{10,... | collective-permute-start | bytes 12296 | tf_op jit(solution)/shard_map/ppermute | solution.py:346
  63.2 3.1 %collective-permute-start.12 = (s32[1,1024]{1,0:T(1,128)S(1)}, s32[1,1024]{1,0:T(1,128)S(1)}, u32[]{:S(2)}, u32[]{:S(2)}) collective-permute-start(s32[1,1024]{1,0:T(1,128)S(1)} %get-tuple-element.18.t0.target_ref), channel_id=1, source_target_pairs={{0,3},{1,0},{2,1},{3,2},{4,7},{5,4},{6,5},{7,6},{8,11},{9,8},{10,9... | collective-permute-start | bytes 12296 | tf_op jit(solution)/shard_map/ppermute | solution.py:346
  71.2 20.0 %all-to-all-start = ((f32[128,1,128]{2,1,0:T(1,128)}), f32[128,1,128]{2,1,0:T(1,128)S(1)}, u32[]{:S(2)}, u32[]{:S(2)}) async-start(f32[128,1,128]{2,1,0:T(1,128)} %bitcast.9), calls=%async_computation | async-start | bytes 131072 | tf_op jit(solution)/shard_map/all_to_all | solution.py:357
  82.4 1.0 copy-start.1
  91.3 1.2 %copy-start.2 = (bf16[2048,256]{1,0:T(8,128)(2,1)S(1)}, bf16[2048,256]{1,0:T(8,128)(2,1)}, u32[]{:S(2)}) copy-start(bf16[2048,256]{1,0:T(8,128)(2,1)} %copy-done.1) | copy-start | bytes 3145732
  98.0 13.9 %all-to-all-start.2 = ((f32[128,1,128]{2,1,0:T(1,128)}), f32[128,1,128]{2,1,0:T(1,128)S(1)}, u32[]{:S(2)}, u32[]{:S(2)}) async-start(f32[128,1,128]{2,1,0:T(1,128)} %bitcast.16), calls=%async_computation.2 | async-start | bytes 131072 | tf_op jit(solution)/shard_map/all_to_all | solution.py:357
where the time goes:
time: 113 us
  starting transfers between devices  45.7 us (40%)
  waiting for transfers between devices  34.4 us (30%)
  Pallas kernels  24.3 us (22%)
  local copies, waits for them, and re-layouts  7.73 us (7%)
    ppermute x12, starting transfers between devices, behind(): lax.ppermute(value, axis, [(i, (i + hop) % size) for i in range(size)])  18.7 us
    all_to_all x2, waiting for transfers between devices, exchange(): lax.all_to_all(sent, ALL, split_axis=0, concat_axis=0, tiled=True)  17.5 us
    ppermute x12, waiting for transfers between devices, behind(): lax.ppermute(value, axis, [(i, (i + hop) % size) for i in range(size)])  16 us
    all_to_all x2, starting transfers between devices, exchange(): lax.all_to_all(sent, ALL, split_axis=0, concat_axis=0, tiled=True)  14.6 us
    all_to_all x1, starting transfers between devices, body(): lax.all_to_all(row_buf.reshape(owners, CAPACITY, width), ALL, split_axis=...  11.5 us
    unnamed x24, local copies, waits for them, and re-layouts  6.9 us
    pallas_call x1, Pallas kernels, margin_pass(): pl.pallas_call(functools.partial(margin_kernel, chunks=chunks), in_specs=...  6.77 us
    pallas_call x1, Pallas kernels, members_pass(): pl.pallas_call(members_kernel, in_specs=[VMEM_SPEC] * 6, out_specs=[VMEM_...  5.5 us
  transfers between devices with their start and end apart: 16, of which 7 were waited for; matrix products, arithmetic and copies ran while one was open for 0% of the time, Pallas kernels for 13%

commit v1 on v0

v1 whole, which is shorter than its diff:
```python
import functools

import jax
import jax.numpy as jnp
from jax import lax
from jax.experimental import pallas as pl
from jax.experimental.pallas import tpu as pltpu
from jax.sharding import Mesh
from jax.sharding import PartitionSpec as P

RIDGE_FIXED = 0.1
STEP_FIXED = 2.0
RIDGE_MEMBER = 0.25
TINY = 1e-30
CG_STEPS = 3
F32 = jnp.float32
BF16 = jnp.bfloat16
LANES = 128
CAPACITY = 16
LEFT, RIGHT, SIDE, MESSAGE = 0, CAPACITY, 2 * CAPACITY, 2 * CAPACITY + 1
ALL = ("z", "y", "core", "feat")
NN = (((1,), (0,)), ((), ()))
NT = (((1,), (1,)), ((), ()))
TN = (((0,), (0,)), ((), ()))
VMEM_SPEC = pl.BlockSpec(memory_space=pltpu.VMEM)


def dot(left, right, dims):
    return lax.dot_general(left, right, dims, preferred_element_type=F32)


def split(value):
    high = value.astype(BF16)
    return high, (value - high.astype(F32)).astype(BF16)


def dot_split(left, high, low, dims):
    left_high, left_low = split(left)
    rows = left.shape[0]
    both = dot(jnp.concatenate([left_high, left_low], axis=0), high, dims)
    return both[:rows] + both[rows:] + dot(left_high, low, dims)


def sublane_iota(shape):
    return lax.broadcasted_iota(jnp.int32, shape, 0)


def lane_iota(shape):
    return lax.broadcasted_iota(jnp.int32, shape, 1)


def hot_rows(count, index):
    shape = (count, index.shape[1])
    return jnp.where(sublane_iota(shape) == index, 1.0, 0.0).astype(BF16)


def per_owner(row):
    return pl.ds(row, LANES, stride=MESSAGE)


def vmem(vmem_mib):
    return pltpu.CompilerParams(vmem_limit_bytes=vmem_mib << 20)


def margin_chunk(weight, feat_ref, start, size):
    columns = feat_ref.shape[1]
    cut = columns // 2
    matrix = dot(weight[:, :cut].astype(BF16), feat_ref[start : start + size, :cut], NT)[0:1]
    sums = []
    for first in range(start, start + size, LANES):
        parts = []
        for sub in range(first, first + LANES, 64):
            total = None
            for column in range(cut, columns, LANES):
                term = feat_ref[sub : sub + 64, column : column + LANES].astype(F32) * weight[
                    0:1, column : column + LANES
                ]
                total = term if total is None else total + term
            parts.append(total)
        sums.append(jnp.sum(jnp.concatenate(parts, axis=0).T, axis=0, keepdims=True))
    return matrix + jnp.concatenate(sums, axis=1)


def front_kernel(
    ids_hbm,
    table_hbm,
    weight_hbm,
    feat_hbm,
    packet_ref,
    feat_ref,
    route_ref,
    ids_ref,
    table_ref,
    weight_ref,
    small_sems,
    feat_sems,
    *,
    mem_dev,
    chunks,
):
    rows = ids_ref.shape[1]
    small = [
        pltpu.make_async_copy(source, target, small_sems.at[i])
        for i, (source, target) in enumerate(
            ((ids_hbm, ids_ref), (table_hbm, table_ref), (weight_hbm, weight_ref))
        )
    ]
    copies = []
    start = 0
    for i, size in enumerate(chunks):
        here = pl.ds(start, size)
        copies.append(pltpu.make_async_copy(feat_hbm.at[here], feat_ref.at[here], feat_sems.at[i]))
        start += size
    for copy in small + copies:
        copy.start()
    for copy in small:
        copy.wait()

    ids = ids_ref[...]
    table = table_ref[...]
    owner_table = (table // mem_dev).astype(F32).astype(BF16)
    slot_table = (table % mem_dev).astype(F32).astype(BF16)
    both = jnp.concatenate([owner_table, slot_table], axis=1)
    found = dot(both, hot_rows(table.shape[0], ids // LANES), TN)
    low_hot = sublane_iota((LANES, rows)) == ids % LANES
    owner = jnp.sum(jnp.where(low_hot, found[:LANES], 0.0), axis=0, keepdims=True)
    slot = jnp.sum(jnp.where(low_hot, found[LANES:], 0.0), axis=0, keepdims=True)
    owner_hot = sublane_iota((LANES, rows)) == owner.astype(jnp.int32)
    hot = jnp.where(owner_hot, 1.0, 0.0).astype(BF16)
    earlier = jnp.where(sublane_iota((rows, rows)) < lane_iota((rows, rows)), 1.0, 0.0).astype(BF16)
    before = dot(hot, earlier, NN)
    rank = jnp.sum(jnp.where(owner_hot, before, 0.0), axis=0, keepdims=True)
    route_ref[0:1, :] = owner
    route_ref[1:2, :] = rank
    route_ref[2:3, :] = slot

    packet_ref[:, feat_ref.shape[0] :] = owner * CAPACITY + rank
    weight = jnp.broadcast_to(weight_ref[...].astype(BF16).astype(F32), (8, weight_ref.shape[1]))
    start = 0
    for copy, size in zip(copies, chunks):
        copy.wait()
        packet_ref[:, start : start + size] = margin_chunk(weight, feat_ref, start, size)
        start += size


def front(ids, table, weight, features, mem_dev):
    rows = ids.shape[1]
    examples, columns = features.shape
    chunks = (examples // 2, examples // 4, examples // 4)
    arguments = (ids, table, weight, features)
    return pl.pallas_call(
        functools.partial(front_kernel, mem_dev=mem_dev, chunks=chunks),
        in_specs=[pl.BlockSpec(memory_space=pl.ANY)] * 4,
        out_specs=[VMEM_SPEC] * 3,
        out_shape=[
            jax.ShapeDtypeStruct((1, examples + rows), F32),
            pltpu.VMEM((examples, columns), BF16),
            pltpu.VMEM((8, rows), F32),
        ],
        scratch_shapes=[
            pltpu.VMEM(ids.shape, jnp.int32),
            pltpu.VMEM(table.shape, jnp.int32),
            pltpu.VMEM(weight.shape, F32),
            pltpu.SemaphoreType.DMA((3,)),
            pltpu.SemaphoreType.DMA((len(chunks),)),
        ],
        compiler_params=vmem(16),
        name="front",
    )(*(pltpu.with_memory_space_constraint(argument, pltpu.HBM) for argument in arguments))


def place_kernel(route_ref, labels_ref, rows_ref, buf_hbm, meta_ref, buf_ref, sem):
    rows, width = rows_ref.shape
    owner = route_ref[0:1, :].astype(jnp.int32)
    rank = route_ref[1:2, :].astype(jnp.int32)
    slot = route_ref[2:3, :]
    first = pl.multiple_of(lax.axis_index("feat") * rows, rows)
    labels = labels_ref[:, pl.ds(first, rows)].astype(F32)
    owner_hot = sublane_iota((LANES, rows)) == owner
    high, low = split(rows_ref[...])
    parts = jnp.concatenate([high, low], axis=1)
    group = 8
    for base in range(0, CAPACITY, group):
        place = [jnp.where(owner_hot & (rank == base + i), 1.0, 0.0).astype(BF16) for i in range(group)]
        moved = dot(jnp.concatenate(place, axis=0), parts, NN)
        moved = moved[:, :width] + moved[:, width:]
        for i in range(group):
            here = slice(i * LANES, (i + 1) * LANES)
            buf_ref[per_owner(LEFT + base + i), :] = moved[here, :LANES]
            buf_ref[per_owner(RIGHT + base + i), :] = moved[here, LANES:]
    buf_ref[per_owner(SIDE), :] = jnp.zeros((LANES, LANES), F32)
    out = pltpu.make_async_copy(buf_ref, buf_hbm, sem)
    out.start()
    slot_hot = jnp.where(owner_hot, slot, 0.0).astype(BF16)
    label_hot = jnp.where(owner_hot, labels, 0.0).astype(BF16)
    meta_ref[...] = dot(slot_hot, hot_rows(LANES, rank + 4 * CAPACITY), NT) + dot(
        label_hot, hot_rows(LANES, rank + 5 * CAPACITY), NT
    )
    out.wait()


def place(routes, labels, member_rows):
    buf = (LANES * MESSAGE, LANES)
    return pl.pallas_call(
        place_kernel,
        in_specs=[VMEM_SPEC] * 3,
        out_specs=[pl.BlockSpec(memory_space=pltpu.HBM), VMEM_SPEC],
        out_shape=[pltpu.HBM(buf, F32), jax.ShapeDtypeStruct((LANES, LANES), F32)],
        scratch_shapes=[pltpu.VMEM(buf, F32), pltpu.SemaphoreType.DMA],
        compiler_params=vmem(16),
        name="place",
    )(routes, labels, member_rows)


def grad_kernel(
    p0, p1, p2, p3, offset_ref, labels_ref, feat_ref, meta_ref, grad_hbm, owner_ref, lane_ref, copies_ref, sem
):
    count = offset_ref.shape[1]
    margin = (p0[:, :count] + p2[:, :count]) + (p1[:, :count] + p3[:, :count]) + offset_ref[...]
    residual = (jax.nn.sigmoid(margin) - labels_ref[...].astype(F32)).astype(BF16)
    grad = dot(jnp.broadcast_to(residual, (8, count)), feat_ref[...], NN)[0:1]
    copies_ref[...] = jnp.broadcast_to(grad[None], copies_ref.shape)
    out = pltpu.make_async_copy(copies_ref, grad_hbm, sem)
    out.start()
    block = p0.shape[1] - count
    for hop, packet_ref in enumerate((p0, p1, p2, p3)):
        number = lax.rem(lax.axis_index("feat") - hop + 4, 4)
        target = packet_ref[:, count:].astype(jnp.int32)
        here = pl.ds(pl.multiple_of(number * block, block), block)
        owner_ref[:, here] = hot_rows(LANES, target // CAPACITY)
        lane_ref[:, here] = hot_rows(LANES, number * CAPACITY + target % CAPACITY)
    out.wait()


def grad_pass(packets, offset, labels, features, meta, peers):
    examples, columns = features.shape
    shape = (peers, 1, columns)
    return pl.pallas_call(
        grad_kernel,
        in_specs=[VMEM_SPEC] * 7 + [pl.BlockSpec(memory_space=pl.ANY)],
        out_specs=[pl.BlockSpec(memory_space=pltpu.HBM), VMEM_SPEC, VMEM_SPEC],
        out_shape=[pltpu.HBM(shape, F32)] + [jax.ShapeDtypeStruct((LANES, examples), BF16)] * 2,
        scratch_shapes=[pltpu.VMEM(shape, F32), pltpu.SemaphoreType.DMA],
        compiler_params=vmem(16),
        name="grad",
    )(*packets, offset, labels, pltpu.with_memory_space_constraint(features, pltpu.VMEM), meta)


def new_kernel(
    grads_ref,
    weight_ref,
    meta_ref,
    owner_ref,
    lane_ref,
    feat_ref,
    buf_hbm,
    updated_ref,
    send_hbm,
    buf_ref,
    sems,
    *,
    examples,
):
    into = pltpu.make_async_copy(buf_hbm, buf_ref, sems.at[0])
    into.start()
    gradient = jnp.sum(grads_ref[...], axis=0) / examples + RIDGE_FIXED * weight_ref[...]
    updated = weight_ref[...] - STEP_FIXED * gradient
    updated_ref[...] = updated
    weight = jnp.broadcast_to(updated.astype(BF16).astype(F32), (8, updated.shape[1]))
    count = feat_ref.shape[0]
    size = 512
    send = meta_ref[...]
    for start in range(0, count, size):
        here = slice(start, start + size)
        high, low = split(margin_chunk(weight, feat_ref, start, size))
        owner_hot = owner_ref[:, here]
        both = dot(jnp.concatenate([owner_hot * high, owner_hot * low], axis=0), lane_ref[:, here], NT)
        send = send + both[:LANES] + both[LANES:]
    into.wait()
    buf_ref[per_owner(SIDE), :] = send
    out = pltpu.make_async_copy(buf_ref, send_hbm, sems.at[1])
    out.start()
    out.wait()


def new_pass(grads, weight, meta, owner_hot, lane_hot, features, row_buf, examples):
    columns = features.shape[1]
    return pl.pallas_call(
        functools.partial(new_kernel, examples=examples),
        in_specs=[VMEM_SPEC] * 6 + [pl.BlockSpec(memory_space=pl.ANY)],
        out_specs=[VMEM_SPEC, pl.BlockSpec(memory_space=pltpu.HBM)],
        out_shape=[jax.ShapeDtypeStruct((1, columns), F32), pltpu.HBM(row_buf.shape, F32)],
        scratch_shapes=[pltpu.VMEM(row_buf.shape, F32), pltpu.SemaphoreType.DMA((2,))],
        compiler_params=vmem(16),
        name="new",
    )(
        grads,
        weight,
        meta,
        owner_hot,
        lane_hot,
        pltpu.with_memory_space_constraint(features, pltpu.VMEM),
        pltpu.with_memory_space_constraint(row_buf, pltpu.HBM),
    )


def to_row(table):
    return jnp.concatenate([table[i : i + 1, :] for i in range(table.shape[0])], axis=1)


def members_kernel(recv_ref, params_ref, counts_ref, out_ref, back_ref, high_ref, low_ref):
    for k in range(CAPACITY):
        rows = jnp.concatenate([recv_ref[per_owner(LEFT + k), :], recv_ref[per_owner(RIGHT + k), :]], axis=1)
        here = pl.ds(k * LANES, LANES)
        high_ref[here, :], low_ref[here, :] = split(rows)
    side = recv_ref[per_owner(SIDE), :].T
    groups = lax.axis_size("feat")
    lane = lane_iota((CAPACITY, LANES))
    offsets = jnp.zeros((CAPACITY, LANES), F32)
    for block in range(groups):
        part = side[block * CAPACITY : (block + 1) * CAPACITY]
        whole = part
        for hop in range(1, groups):
            whole = whole + pltpu.roll(part, hop, 1)
        whole = pltpu.roll(whole, (block - groups + 1) % LANES, 1)
        offsets = jnp.where(lane % groups == block, whole, offsets)
    offset = to_row(offsets)
    slot = to_row(side[4 * CAPACITY : 5 * CAPACITY]).astype(jnp.int32)
    label = to_row(side[5 * CAPACITY : 6 * CAPACITY])
    members = params_ref.shape[0]
    mask = sublane_iota((members, slot.shape[1])) == slot

    def own(value):
        return jnp.sum(jnp.where(mask, value, 0.0), axis=0, keepdims=True)

    high, low = high_ref[...], low_ref[...]
    old = params_ref[...]
    scaling = 1.0 / (counts_ref[...].astype(F32) + 1.0)
    margin = offset + own(dot_split(old, high, low, NT))
    probability = jax.nn.sigmoid(margin)
    weight = probability * (1.0 - probability)
    errors = jnp.where(mask, label - probability, 0.0)
    remains = scaling * dot_split(errors, high, low, NN) - RIDGE_MEMBER * old
    direction = remains
    delta = jnp.zeros_like(remains)
    norm_now = jnp.sum(remains * remains, axis=1, keepdims=True)
    for step in range(CG_STEPS):
        along = jnp.where(mask, dot_split(direction, high, low, NT), 0.0)
        weighted = along * weight
        curve = scaling * jnp.sum(weighted * along, axis=1, keepdims=True) + RIDGE_MEMBER * jnp.sum(
            direction * direction, axis=1, keepdims=True
        )
        step_size = norm_now / (curve + TINY)
        delta = delta + step_size * direction
        margin = margin + jnp.sum(along * step_size, axis=0, keepdims=True)
        if step < CG_STEPS - 1:
            image = scaling * dot_split(weighted, high, low, NN) + RIDGE_MEMBER * direction
            remains = remains - step_size * image
            norm_next = jnp.sum(remains * remains, axis=1, keepdims=True)
            direction = remains + (norm_next / (norm_now + TINY)) * direction
            norm_now = norm_next
    out_ref[...] = old + delta
    table = jnp.concatenate(
        [margin[:, k * LANES : (k + 1) * LANES] for k in range(CAPACITY)]
        + [jnp.zeros((LANES - CAPACITY, LANES), F32)],
        axis=0,
    )
    back_ref[...] = table.T


def members_pass(recv, member_params, counts):
    members, width = member_params.shape
    held = pltpu.VMEM((LANES * CAPACITY, width), BF16)
    return pl.pallas_call(
        members_kernel,
        in_specs=[VMEM_SPEC] * 3,
        out_specs=[VMEM_SPEC] * 2,
        out_shape=[
            jax.ShapeDtypeStruct(member_params.shape, F32),
            jax.ShapeDtypeStruct((LANES, LANES), F32),
        ],
        scratch_shapes=[held, held],
        compiler_params=vmem(16),
        name="members",
    )(recv, member_params, counts)


def collect_kernel(back_ref, route_ref, out_ref):
    high, low = split(back_ref[...])
    hot = hot_rows(LANES, route_ref[0:1, :].astype(jnp.int32))
    found = dot(high, hot, TN) + dot(low, hot, TN)
    here = sublane_iota(found.shape) == route_ref[1:2, :].astype(jnp.int32)
    out_ref[...] = jnp.sum(jnp.where(here, found, 0.0), axis=0, keepdims=True)


def collect(back, routes):
    return pl.pallas_call(
        collect_kernel,
        in_specs=[VMEM_SPEC] * 2,
        out_specs=VMEM_SPEC,
        out_shape=jax.ShapeDtypeStruct((1, routes.shape[1]), F32),
        compiler_params=vmem(8),
        name="collect",
    )(back, routes)


def behind(value, axis):
    size = lax.axis_size(axis)
    return [value] + [
        lax.ppermute(value, axis, [(i, (i + hop) % size) for i in range(size)])
        for hop in range(1, size)
    ]


def gather(copies, axes):
    return lax.all_to_all(copies, axes, split_axis=0, concat_axis=0, tiled=True)


def exchange(table):
    sent = table.reshape(LANES, 1, -1)
    got = lax.all_to_all(sent, ALL, split_axis=0, concat_axis=0, tiled=True)
    return got.reshape(table.shape)


def body(
    features,
    fixed_weight,
    prior_offset,
    labels,
    impression_member,
    member_position,
    member_counts,
    member_features,
    member_params,
):
    owners = lax.axis_size(ALL)
    mem_dev = member_params.shape[0]
    examples = features.shape[0] * owners // lax.axis_size("feat")
    weight = fixed_weight[None]
    label_row = labels[None]

    packet, held, routes = front(
        impression_member[None],
        member_position.reshape(-1, LANES),
        weight,
        features,
        mem_dev,
    )
    packets = behind(packet, "feat")
    row_buf, meta = place(routes, label_row, member_features)
    dp = ("z", "y", "core")
    grad, owner_hot, lane_hot = grad_pass(
        packets, prior_offset[None], label_row, held, meta, lax.axis_size(dp)
    )
    grads = gather(grad, dp)
    updated, send = new_pass(grads, weight, meta, owner_hot, lane_hot, held, row_buf, examples)
    updated_params, back = members_pass(exchange(send), member_params, member_counts[:, None])
    total = collect(exchange(back), routes)
    return updated[0], updated_params, total[0]


def solution(mesh):
    split_mesh = Mesh(mesh.devices.reshape(4, 4, 2, 4), ALL)
    dp = ("z", "y", "core")
    placed = (
        P(dp, "feat"),
        P("feat"),
        P(dp),
        P(dp),
        P(ALL),
        P(),
        P(ALL),
        P(ALL, None),
        P(ALL, None),
    )
    return jax.shard_map(
        body,
        mesh=split_mesh,
        in_specs=placed,
        out_specs=(P("feat"), P(ALL, None), P(ALL)),
        check_vma=False,
    )
```

time: 113 us -> 104 us (0.920)
  starting transfers between devices: 45.7 us -> 9.43 us
  blocking collectives: 0 us -> 31.6 us
  local copies, waits for them, and re-layouts: 7.73 us -> 0.12 us
  Pallas kernels: 24.3 us -> 29.8 us
  waiting for transfers between devices: 34.4 us -> 31.6 us
    all_to_all x0 -> x2, blocking collectives: none -> 31.6 us  [the longest x1 18.5 us: gather(): return lax.all_to_all(copies, axes, split_axis=0, concat_axis=0, tiled=True)]
    all_to_all x3 -> x1, starting transfers between devices: 26.1 us -> 3.72 us  [exchange(): got = lax.all_to_all(sent, ALL, split_axis=0, concat_axis=0, tiled=True)]
    ppermute x12 -> x3, waiting for transfers between devices: 16 us -> 0.01 us  [behind(): lax.ppermute(value, axis, [(i, (i + hop) % size) for i in range(size)])]
    all_to_all x3 -> x1, waiting for transfers between devices: 17.5 us -> 31.5 us  [exchange(): got = lax.all_to_all(sent, ALL, split_axis=0, concat_axis=0, tiled=True)]
    ppermute x12 -> x3, starting transfers between devices: 18.7 us -> 5.71 us  [behind(): lax.ppermute(value, axis, [(i, (i + hop) % size) for i in range(size)])]
    unnamed x24 -> x12, local copies, waits for them, and re-layouts: 6.9 us -> 0.03 us
    pallas_call x6 -> x5, Pallas kernels: 19.4 us -> 23 us  [the longest x1 7.91 us: front(): pl.pallas_call(functools.partial(front_kernel, mem_dev=mem_dev, chunks=ch...]
    pallas_call x1, Pallas kernels: 4.87 us -> 6.82 us  [new_pass(): pl.pallas_call(functools.partial(new_kernel, examples=examples), in_specs...]
  transfers between devices with their start and end apart: 16 -> 4, of which waited for: 7 -> 1; matrix products, arithmetic and copies ran while one was open for 0% -> 0% of each run, Pallas kernels for 13% -> 4%
where the time goes in v1:
time: 104 us; the launch traced here: 103 us
  waiting for transfers between devices  31.6 us (30%)
  blocking collectives  31.6 us (30%)
  Pallas kernels  29.8 us (29%)
  starting transfers between devices  9.43 us (9%)
    all_to_all x1, waiting for transfers between devices, exchange(): got = lax.all_to_all(sent, ALL, split_axis=0, concat_axis=0, tiled=True)  31.5 us
    all_to_all x1, blocking collectives, gather(): return lax.all_to_all(copies, axes, split_axis=0, concat_axis=0, tiled=True)  18.5 us
    all_to_all x1, blocking collectives, exchange(): got = lax.all_to_all(sent, ALL, split_axis=0, concat_axis=0, tiled=True)  13 us
    pallas_call x1, Pallas kernels, front(): pl.pallas_call(functools.partial(front_kernel, mem_dev=mem_dev, chunks=ch...  7.91 us
    pallas_call x1, Pallas kernels, new_pass(): pl.pallas_call(functools.partial(new_kernel, examples=examples), in_specs...  6.82 us
    pallas_call x1, Pallas kernels, members_pass(): pl.pallas_call(members_kernel, in_specs=[VMEM_SPEC] * 3, out_specs=[VMEM_...  6.52 us
    ppermute x3, starting transfers between devices, behind(): lax.ppermute(value, axis, [(i, (i + hop) % size) for i in range(size)])  5.71 us
    pallas_call x1, Pallas kernels, place(): pl.pallas_call(place_kernel, in_specs=[VMEM_SPEC] * 3, out_specs=[pl.Bloc...  3.84 us
  transfers between devices with their start and end apart: 4, of which 1 were waited for; matrix products, arithmetic and copies ran while one was open for 0% of the time, Pallas kernels for 4%

profile of v1, /device:TPU:1, one launch (start us, length us, event | category | flops | bytes accessed | tf_op | source)
XLA Modules:
  0.0 103.2 jit_solution(8045367541471777213)
XLA Ops:
  0.6 0.0 copy-start
  0.6 0.0 copy-start.1
  0.7 0.0 copy-start.4
  0.7 7.9 %front.1 = (f32[1,5120]{1,0:T(1,128)S(1)}, bf16[4096,2048]{1,0:T(8,128)(2,1)S(1)}, f32[8,1024]{1,0:T(8,128)S(1)}) custom-call(s32[1,1024]{1,0:T(1,128)} %bitcast.24, s32[32,128]{1,0:T(8,128)} %bitcast.23, f32[1,2048]{1,0:T(1,128)} %bitcast.19, bf16[4096,2048]{1,0:T(8,128)(2,1)} %feat_hbm.1), custom_call_target="tpu_custom_call" | custom-call | tf_op jit(solution)/shard_map/front/pallas_call | solution.py:151
  8.6 2.1 %collective-permute-start = (f32[1,5120]{1,0:T(1,128)S(1)}, f32[1,5120]{1,0:T(1,128)S(1)}, u32[]{:S(2)}, u32[]{:S(2)}) collective-permute-start(f32[1,5120]{1,0:T(1,128)S(1)} %get-tuple-element.15.p0), channel_id=1, source_target_pairs={{0,1},{1,2},{2,3},{3,0},{4,5},{5,6},{6,7},{7,4},{8,9},{9,10},{10,1... | collective-permute-start | bytes 61448 | tf_op jit(solution)/shard_map/ppermute | solution.py:410
  10.7 2.5 %collective-permute-start.1 = (f32[1,5120]{1,0:T(1,128)S(1)}, f32[1,5120]{1,0:T(1,128)S(1)}, u32[]{:S(2)}, u32[]{:S(2)}) collective-permute-start(f32[1,5120]{1,0:T(1,128)S(1)} %get-tuple-element.15.p0), channel_id=1, source_target_pairs={{0,2},{1,3},{2,0},{3,1},{4,6},{5,7},{6,4},{7,5},{8,10},{9,11},{10,... | collective-permute-start | bytes 61448 | tf_op jit(solution)/shard_map/ppermute | solution.py:410
  13.1 1.2 %collective-permute-start.2 = (f32[1,5120]{1,0:T(1,128)S(1)}, f32[1,5120]{1,0:T(1,128)S(1)}, u32[]{:S(2)}, u32[]{:S(2)}) collective-permute-start(f32[1,5120]{1,0:T(1,128)S(1)} %get-tuple-element.15.p0), channel_id=1, source_target_pairs={{0,3},{1,0},{2,1},{3,2},{4,7},{5,4},{6,5},{7,6},{8,11},{9,8},{10,9... | collective-permute-start | bytes 61448 | tf_op jit(solution)/shard_map/ppermute | solution.py:410
  14.3 0.0 copy-done
  14.3 0.0 copy-done.1
  14.3 3.8 %place.1 = (f32[4224,128]{1,0:T(8,128)}, f32[128,128]{1,0:T(8,128)S(1)}) custom-call(f32[8,1024]{1,0:T(8,128)S(1)} %get-tuple-element.17.route_ref, s32[1,4096]{1,0:T(1,128)S(1)} %bitcast.16, f32[1024,256]{1,0:T(8,128)S(1)} %copy-done), custom_call_target="tpu_custom_call" | custom-call | tf_op jit(solution)/shard_map/place/pallas_call | solution.py:204
  18.1 0.0 collective-permute-done.p1
  18.2 0.0 collective-permute-done.1.p2
  18.2 0.0 collective-permute-done.2.p3
  18.2 0.0 copy-done.4
  18.2 0.0 copy-start.2
  18.2 3.8 %grad.1 = (f32[32,1,2048]{2,1,0:T(1,128)}, bf16[128,4096]{1,0:T(8,128)(2,1)S(1)}, bf16[128,4096]{1,0:T(8,128)(2,1)S(1)}) custom-call(f32[1,5120]{1,0:T(1,128)S(1)} %get-tuple-element.15.p0, f32[1,5120]{1,0:T(1,128)S(1)} %collective-permute-done.p1, f32[1,5120]{1,0:T(1,128)S(1)} %collective-permute-done.1.p2, f32[1,5120]{1,0:T(1,128)S(1)} %collective-permute-done.2.p3, ...), custom_call_target="tpu_custom_call" | custom-call | tf_op jit(solution)/shard_map/grad/pallas_call | solution.py:238
  22.0 18.5 %all_to_all.15.grads_ref = f32[32,1,2048]{2,1,0:T(1,128)S(1)} all-to-all(f32[32,1,2048]{2,1,0:T(1,128)} %get-tuple-element.19), channel_id=1, replica_groups=mesh['z'=4,'y'=4,'core'=2,'feat'=4] {'z','y','core'}, dimensions={0} | all-to-all | bytes 524288 | tf_op jit(solution)/shard_map/all_to_all | solution.py:416
  40.5 0.0 copy-done.2
  40.5 6.8 %new.1 = (f32[1,2048]{1,0:T(1,128)}, f32[4224,128]{1,0:T(8,128)}) custom-call(f32[32,1,2048]{2,1,0:T(1,128)S(1)} %all_to_all.15.grads_ref, f32[1,2048]{1,0:T(1,128)S(1)} %bitcast.20, f32[128,128]{1,0:T(8,128)S(1)} %get-tuple-element.18.meta_ref, bf16[128,4096]{1,0:T(8,128)(2,1)S(1)} %get-tuple-element.20.owner_ref, ...), custom_call_target="tpu_custom_call" | custom-call | tf_op jit(solution)/shard_map/new/pallas_call | solution.py:288
  47.3 0.0 copy-start.5
  47.3 0.0 copy-start.3
  47.4 3.7 %all-to-all-start.1 = ((f32[128,1,4224]{2,1,0:T(1,128)}), f32[128,1,4224]{2,1,0:T(1,128)S(1)}, u32[]{:S(2)}, u32[]{:S(2)}) async-start(f32[128,1,4224]{2,1,0:T(1,128)} %bitcast.22), calls=%async_computation.1 | async-start | bytes 4325376 | tf_op jit(solution)/shard_map/all_to_all | solution.py:421
  51.1 0.0 copy-done.5
  51.1 0.1 copy.14.counts_ref
  51.2 31.5 %all-to-all-done.1 = f32[128,1,4224]{2,1,0:T(1,128)S(1)} async-done(((f32[128,1,4224]{2,1,0:T(1,128)}), f32[128,1,4224]{2,1,0:T(1,128)S(1)}, u32[]{:S(2)}, u32[]{:S(2)}) %all-to-all-start.1) | async-done | bytes 2162720 | tf_op jit(solution)/shard_map/all_to_all | solution.py:421
  82.7 0.0 copy-done.3
  82.7 6.5 %members.1 = (f32[32,256]{1,0:T(8,128)}, f32[128,128]{1,0:T(8,128)S(1)}) custom-call(f32[4224,128]{1,0:T(8,128)S(1)} %bitcast.14, f32[32,256]{1,0:T(8,128)S(1)} %copy-done.3, s32[32,1]{1,0:T(8,128)S(1)} %copy.14.counts_ref), custom_call_target="tpu_custom_call" | custom-call | tf_op jit(solution)/shard_map/members/pallas_call | solution.py:374
  89.3 13.0 %all_to_all.16 = f32[128,1,128]{2,1,0:T(1,128)S(1)} all-to-all(f32[128,1,128]{2,1,0:T(1,128)S(1)} %bitcast.18), channel_id=1, replica_groups=mesh['z'=4,'y'=4,'core'=2,'feat'=4] {'z','y','core','feat'}, dimensions={0} | all-to-all | bytes 131072 | tf_op jit(solution)/shard_map/all_to_all | solution.py:421
  102.3 0.9 collect.1
Async XLA Ops:
  0.6 13.7 %copy-start = (f32[1024,256]{1,0:T(8,128)S(1)}, f32[1024,256]{1,0:T(8,128)}, u32[]{:S(2)}) copy-start(f32[1024,256]{1,0:T(8,128)} %rows_ref.1) | copy-start | bytes 3145732
  0.6 13.7 %copy-start.1 = (s32[4096]{0:T(1024)S(1)}, s32[4096]{0:T(1024)}, u32[]{:S(2)}) copy-start(s32[4096]{0:T(1024)} %param.12) | copy-start | bytes 49156
  0.7 17.5 %copy-start.4 = (f32[4096]{0:T(1024)S(1)}, f32[4096]{0:T(1024)}, u32[]{:S(2)}) copy-start(f32[4096]{0:T(1024)} %param.11) | copy-start | bytes 49156
  8.6 9.6 %collective-permute-start = (f32[1,5120]{1,0:T(1,128)S(1)}, f32[1,5120]{1,0:T(1,128)S(1)}, u32[]{:S(2)}, u32[]{:S(2)}) collective-permute-start(f32[1,5120]{1,0:T(1,128)S(1)} %get-tuple-element.15.p0), channel_id=1, source_target_pairs={{0,1},{1,2},{2,3},{3,0},{4,5},{5,6},{6,7},{7,4},{8,9},{9,10},{10,1... | collective-permute-start | bytes 61448 | tf_op jit(solution)/shard_map/ppermute | solution.py:410
  10.7 7.5 %collective-permute-start.1 = (f32[1,5120]{1,0:T(1,128)S(1)}, f32[1,5120]{1,0:T(1,128)S(1)}, u32[]{:S(2)}, u32[]{:S(2)}) collective-permute-start(f32[1,5120]{1,0:T(1,128)S(1)} %get-tuple-element.15.p0), channel_id=1, source_target_pairs={{0,2},{1,3},{2,0},{3,1},{4,6},{5,7},{6,4},{7,5},{8,10},{9,11},{10,... | collective-permute-start | bytes 61448 | tf_op jit(solution)/shard_map/ppermute | solution.py:410
  13.1 5.0 %collective-permute-start.2 = (f32[1,5120]{1,0:T(1,128)S(1)}, f32[1,5120]{1,0:T(1,128)S(1)}, u32[]{:S(2)}, u32[]{:S(2)}) collective-permute-start(f32[1,5120]{1,0:T(1,128)S(1)} %get-tuple-element.15.p0), channel_id=1, source_target_pairs={{0,3},{1,0},{2,1},{3,2},{4,7},{5,4},{6,5},{7,6},{8,11},{9,8},{10,9... | collective-permute-start | bytes 61448 | tf_op jit(solution)/shard_map/ppermute | solution.py:410
  18.2 22.3 %copy-start.2 = (f32[2048]{0:T(1024)S(1)}, f32[2048]{0:T(1024)}, u32[]{:S(2)}) copy-start(f32[2048]{0:T(1024)} %param.10) | copy-start | bytes 24580
  47.3 3.8 %copy-start.5 = (s32[32]{0:T(128)S(1)}, s32[32]{0:T(128)}, u32[]{:S(2)}) copy-start(s32[32]{0:T(128)} %param.15) | copy-start | bytes 388
  47.3 35.4 %copy-start.3 = (f32[32,256]{1,0:T(8,128)S(1)}, f32[32,256]{1,0:T(8,128)}, u32[]{:S(2)}) copy-start(f32[32,256]{1,0:T(8,128)} %params_ref.1) | copy-start | bytes 98308
  47.4 35.4 %all-to-all-start.1 = ((f32[128,1,4224]{2,1,0:T(1,128)}), f32[128,1,4224]{2,1,0:T(1,128)S(1)}, u32[]{:S(2)}, u32[]{:S(2)}) async-start(f32[128,1,4224]{2,1,0:T(1,128)} %bitcast.22), calls=%async_computation.1 | async-start | bytes 4325376 | tf_op jit(solution)/shard_map/all_to_all | solution.py:421

commit v2 on v1

--- a/solution.py
+++ b/solution.py
@@ -38,7 +38,8 @@
     left_high, left_low = split(left)
     rows = left.shape[0]
     both = dot(jnp.concatenate([left_high, left_low], axis=0), high, dims)
-    return both[:rows] + both[rows:] + dot(left_high, low, dims)
+    total = both[:rows] + both[rows:]
+    return total if low is None else total + dot(left_high, low, dims)
 
 
 def sublane_iota(shape):
@@ -50,8 +51,16 @@
 
 
 def hot_rows(count, index):
-    shape = (count, index.shape[1])
-    return jnp.where(sublane_iota(shape) == index, 1.0, 0.0).astype(BF16)
+    number = sublane_iota((count, LANES)).astype(F32).astype(BF16)
+    index = index.astype(F32).astype(BF16)
+    one, zero = jnp.ones((), BF16), jnp.zeros((), BF16)
+    return jnp.concatenate(
+        [
+            jnp.where(number == index[:, start : start + LANES], one, zero)
+            for start in range(0, index.shape[1], LANES)
+        ],
+        axis=1,
+    )
 
 
 def per_owner(row):
@@ -146,7 +155,7 @@
 def front(ids, table, weight, features, mem_dev):
     rows = ids.shape[1]
     examples, columns = features.shape
-    chunks = (examples // 2, examples // 4, examples // 4)
+    chunks = (examples // 2, examples // 2)
     arguments = (ids, table, weight, features)
     return pl.pallas_call(
         functools.partial(front_kernel, mem_dev=mem_dev, chunks=chunks),
@@ -169,19 +178,19 @@
     )(*(pltpu.with_memory_space_constraint(argument, pltpu.HBM) for argument in arguments))
 
 
-def place_kernel(route_ref, labels_ref, rows_ref, buf_hbm, meta_ref, buf_ref, sem):
+def place_kernel(route_ref, labels_ref, rows_ref, buf_ref, meta_ref):
     rows, width = rows_ref.shape
     owner = route_ref[0:1, :].astype(jnp.int32)
     rank = route_ref[1:2, :].astype(jnp.int32)
     slot = route_ref[2:3, :]
     first = pl.multiple_of(lax.axis_index("feat") * rows, rows)
     labels = labels_ref[:, pl.ds(first, rows)].astype(F32)
-    owner_hot = sublane_iota((LANES, rows)) == owner
+    owner_hot = hot_rows(LANES, owner)
     high, low = split(rows_ref[...])
     parts = jnp.concatenate([high, low], axis=1)
     group = 8
     for base in range(0, CAPACITY, group):
-        place = [jnp.where(owner_hot & (rank == base + i), 1.0, 0.0).astype(BF16) for i in range(group)]
+        place = [owner_hot * jnp.where(rank == base + i, 1.0, 0.0).astype(BF16) for i in range(group)]
         moved = dot(jnp.concatenate(place, axis=0), parts, NN)
         moved = moved[:, :width] + moved[:, width:]
         for i in range(group):
@@ -189,14 +198,11 @@
             buf_ref[per_owner(LEFT + base + i), :] = moved[here, :LANES]
             buf_ref[per_owner(RIGHT + base + i), :] = moved[here, LANES:]
     buf_ref[per_owner(SIDE), :] = jnp.zeros((LANES, LANES), F32)
-    out = pltpu.make_async_copy(buf_ref, buf_hbm, sem)
-    out.start()
-    slot_hot = jnp.where(owner_hot, slot, 0.0).astype(BF16)
-    label_hot = jnp.where(owner_hot, labels, 0.0).astype(BF16)
+    slot_hot = owner_hot * slot.astype(BF16)
+    label_hot = owner_hot * labels.astype(BF16)
     meta_ref[...] = dot(slot_hot, hot_rows(LANES, rank + 4 * CAPACITY), NT) + dot(
         label_hot, hot_rows(LANES, rank + 5 * CAPACITY), NT
     )
-    out.wait()
 
 
 def place(routes, labels, member_rows):
@@ -204,24 +210,35 @@
     return pl.pallas_call(
         place_kernel,
         in_specs=[VMEM_SPEC] * 3,
-        out_specs=[pl.BlockSpec(memory_space=pltpu.HBM), VMEM_SPEC],
-        out_shape=[pltpu.HBM(buf, F32), jax.ShapeDtypeStruct((LANES, LANES), F32)],
-        scratch_shapes=[pltpu.VMEM(buf, F32), pltpu.SemaphoreType.DMA],
+        out_specs=[VMEM_SPEC] * 2,
+        out_shape=[pltpu.VMEM(buf, F32), jax.ShapeDtypeStruct((LANES, LANES), F32)],
         compiler_params=vmem(16),
         name="place",
     )(routes, labels, member_rows)
 
 
+def to_row(table):
+    return jnp.concatenate([table[i : i + 1, :] for i in range(table.shape[0])], axis=1)
+
+
+def to_table(row):
+    return jnp.concatenate([row[:, i : i + LANES] for i in range(0, row.shape[1], LANES)], axis=0)
+
+
 def grad_kernel(
-    p0, p1, p2, p3, offset_ref, labels_ref, feat_ref, meta_ref, grad_hbm, owner_ref, lane_ref, copies_ref, sem
+    p0,
+    p1,
+    p2,
+    p3,
+    offset_ref,
+    labels_ref,
+    feat_ref,
+    meta_ref,
+    copies_ref,
+    owner_ref,
+    lane_ref,
 ):
     count = offset_ref.shape[1]
-    margin = (p0[:, :count] + p2[:, :count]) + (p1[:, :count] + p3[:, :count]) + offset_ref[...]
-    residual = (jax.nn.sigmoid(margin) - labels_ref[...].astype(F32)).astype(BF16)
-    grad = dot(jnp.broadcast_to(residual, (8, count)), feat_ref[...], NN)[0:1]
-    copies_ref[...] = jnp.broadcast_to(grad[None], copies_ref.shape)
-    out = pltpu.make_async_copy(copies_ref, grad_hbm, sem)
-    out.start()
     block = p0.shape[1] - count
     for hop, packet_ref in enumerate((p0, p1, p2, p3)):
         number = lax.rem(lax.axis_index("feat") - hop + 4, 4)
@@ -229,21 +246,29 @@
         here = pl.ds(pl.multiple_of(number * block, block), block)
         owner_ref[:, here] = hot_rows(LANES, target // CAPACITY)
         lane_ref[:, here] = hot_rows(LANES, number * CAPACITY + target % CAPACITY)
-    out.wait()
+    margin = (p0[:, :count] + p2[:, :count]) + (p1[:, :count] + p3[:, :count]) + offset_ref[...]
+    residual = (jax.nn.sigmoid(margin) - labels_ref[...].astype(F32)).astype(BF16)
+    grad = dot(jnp.broadcast_to(residual, (8, count)), feat_ref[...], NN)[0:1]
+    copies_ref[...] = jnp.broadcast_to(to_table(grad)[None], copies_ref.shape)
 
 
 def grad_pass(packets, offset, labels, features, meta, peers):
     examples, columns = features.shape
-    shape = (peers, 1, columns)
+    shape = (peers, columns // LANES, LANES)
     return pl.pallas_call(
         grad_kernel,
         in_specs=[VMEM_SPEC] * 7 + [pl.BlockSpec(memory_space=pl.ANY)],
-        out_specs=[pl.BlockSpec(memory_space=pltpu.HBM), VMEM_SPEC, VMEM_SPEC],
-        out_shape=[pltpu.HBM(shape, F32)] + [jax.ShapeDtypeStruct((LANES, examples), BF16)] * 2,
-        scratch_shapes=[pltpu.VMEM(shape, F32), pltpu.SemaphoreType.DMA],
+        out_specs=[VMEM_SPEC] * 3,
+        out_shape=[pltpu.VMEM(shape, F32)] + [pltpu.VMEM((LANES, examples), BF16)] * 2,
         compiler_params=vmem(16),
         name="grad",
-    )(*packets, offset, labels, pltpu.with_memory_space_constraint(features, pltpu.VMEM), meta)
+    )(
+        *packets,
+        offset,
+        labels,
+        pltpu.with_memory_space_constraint(features, pltpu.VMEM),
+        meta,
+    )
 
 
 def new_kernel(
@@ -253,19 +278,19 @@
     owner_ref,
     lane_ref,
     feat_ref,
-    buf_hbm,
+    buf_ref,
+    updated_hbm,
+    send_ref,
     updated_ref,
-    send_hbm,
-    buf_ref,
-    sems,
+    sem,
     *,
     examples,
 ):
-    into = pltpu.make_async_copy(buf_hbm, buf_ref, sems.at[0])
-    into.start()
-    gradient = jnp.sum(grads_ref[...], axis=0) / examples + RIDGE_FIXED * weight_ref[...]
+    gradient = to_row(jnp.sum(grads_ref[...], axis=0)) / examples + RIDGE_FIXED * weight_ref[...]
     updated = weight_ref[...] - STEP_FIXED * gradient
     updated_ref[...] = updated
+    result = pltpu.make_async_copy(updated_ref, updated_hbm, sem)
+    result.start()
     weight = jnp.broadcast_to(updated.astype(BF16).astype(F32), (8, updated.shape[1]))
     count = feat_ref.shape[0]
     size = 512
@@ -276,21 +301,19 @@
         owner_hot = owner_ref[:, here]
         both = dot(jnp.concatenate([owner_hot * high, owner_hot * low], axis=0), lane_ref[:, here], NT)
         send = send + both[:LANES] + both[LANES:]
-    into.wait()
-    buf_ref[per_owner(SIDE), :] = send
-    out = pltpu.make_async_copy(buf_ref, send_hbm, sems.at[1])
-    out.start()
-    out.wait()
+    send_ref[per_owner(SIDE), :] = send
+    result.wait()
 
 
 def new_pass(grads, weight, meta, owner_hot, lane_hot, features, row_buf, examples):
     columns = features.shape[1]
     return pl.pallas_call(
         functools.partial(new_kernel, examples=examples),
-        in_specs=[VMEM_SPEC] * 6 + [pl.BlockSpec(memory_space=pl.ANY)],
-        out_specs=[VMEM_SPEC, pl.BlockSpec(memory_space=pltpu.HBM)],
-        out_shape=[jax.ShapeDtypeStruct((1, columns), F32), pltpu.HBM(row_buf.shape, F32)],
-        scratch_shapes=[pltpu.VMEM(row_buf.shape, F32), pltpu.SemaphoreType.DMA((2,))],
+        in_specs=[VMEM_SPEC] * 7,
+        out_specs=[pl.BlockSpec(memory_space=pltpu.HBM), VMEM_SPEC],
+        out_shape=[pltpu.HBM((1, columns), F32), pltpu.VMEM(row_buf.shape, F32)],
+        input_output_aliases={6: 1},
+        scratch_shapes=[pltpu.VMEM((1, columns), F32), pltpu.SemaphoreType.DMA],
         compiler_params=vmem(16),
         name="new",
     )(
@@ -300,15 +323,15 @@
         owner_hot,
         lane_hot,
         pltpu.with_memory_space_constraint(features, pltpu.VMEM),
-        pltpu.with_memory_space_constraint(row_buf, pltpu.HBM),
-    )
-
-
-def to_row(table):
-    return jnp.concatenate([table[i : i + 1, :] for i in range(table.shape[0])], axis=1)
-
-
-def members_kernel(recv_ref, params_ref, counts_ref, out_ref, back_ref, high_ref, low_ref):
+        pltpu.with_memory_space_constraint(row_buf, pltpu.VMEM),
+    )
+
+
+def members_kernel(
+    recv_ref, params_ref, counts_ref, route_hbm, out_ref, back_ref, route_ref, high_ref, low_ref, sem
+):
+    keep = pltpu.make_async_copy(route_hbm, route_ref, sem)
+    keep.start()
     for k in range(CAPACITY):
         rows = jnp.concatenate([recv_ref[per_owner(LEFT + k), :], recv_ref[per_owner(RIGHT + k), :]], axis=1)
         here = pl.ds(k * LANES, LANES)
@@ -335,7 +358,9 @@
 
     high, low = high_ref[...], low_ref[...]
     old = params_ref[...]
-    scaling = 1.0 / (counts_ref[...].astype(F32) + 1.0)
+    diagonal = sublane_iota((members, members)) == lane_iota((members, members))
+    scales = jnp.broadcast_to(1.0 / (counts_ref[...].astype(F32) + 1.0), (members, members))
+    scaling = jnp.sum(jnp.where(diagonal, scales, 0.0), axis=1, keepdims=True)
     margin = offset + own(dot_split(old, high, low, NT))
     probability = jax.nn.sigmoid(margin)
     weight = probability * (1.0 - probability)
@@ -345,7 +370,7 @@
     delta = jnp.zeros_like(remains)
     norm_now = jnp.sum(remains * remains, axis=1, keepdims=True)
     for step in range(CG_STEPS):
-        along = jnp.where(mask, dot_split(direction, high, low, NT), 0.0)
+        along = jnp.where(mask, dot_split(direction, high, None if step == 2 else low, NT), 0.0)
         weighted = along * weight
         curve = scaling * jnp.sum(weighted * along, axis=1, keepdims=True) + RIDGE_MEMBER * jnp.sum(
             direction * direction, axis=1, keepdims=True
@@ -354,7 +379,7 @@
         delta = delta + step_size * direction
         margin = margin + jnp.sum(along * step_size, axis=0, keepdims=True)
         if step < CG_STEPS - 1:
-            image = scaling * dot_split(weighted, high, low, NN) + RIDGE_MEMBER * direction
+            image = scaling * dot_split(weighted, high, None if step == 1 else low, NN) + RIDGE_MEMBER * direction
             remains = remains - step_size * image
             norm_next = jnp.sum(remains * remains, axis=1, keepdims=True)
             direction = remains + (norm_next / (norm_now + TINY)) * direction
@@ -366,42 +391,51 @@
         axis=0,
     )
     back_ref[...] = table.T
-
-
-def members_pass(recv, member_params, counts):
+    keep.wait()
+
+
+def members_pass(recv, member_params, counts, routes):
     members, width = member_params.shape
     held = pltpu.VMEM((LANES * CAPACITY, width), BF16)
     return pl.pallas_call(
         members_kernel,
-        in_specs=[VMEM_SPEC] * 3,
-        out_specs=[VMEM_SPEC] * 2,
+        in_specs=[VMEM_SPEC] * 3 + [pl.BlockSpec(memory_space=pl.ANY)],
+        out_specs=[VMEM_SPEC] * 3,
         out_shape=[
-            jax.ShapeDtypeStruct(member_params.shape, F32),
+            pltpu.VMEM(member_params.shape, F32),
             jax.ShapeDtypeStruct((LANES, LANES), F32),
+            pltpu.VMEM(routes.shape, F32),
         ],
-        scratch_shapes=[held, held],
+        scratch_shapes=[held, held, pltpu.SemaphoreType.DMA],
         compiler_params=vmem(16),
         name="members",
-    )(recv, member_params, counts)
-
-
-def collect_kernel(back_ref, route_ref, out_ref):
-    high, low = split(back_ref[...])
+    )(recv, member_params, counts, routes)
+
+
+def collect_kernel(back_ref, route_ref, params_ref, out_ref, params_hbm, sem):
+    result = pltpu.make_async_copy(params_ref, params_hbm, sem)
+    result.start()
+    high, low = split(back_ref[:, :CAPACITY])
     hot = hot_rows(LANES, route_ref[0:1, :].astype(jnp.int32))
-    found = dot(high, hot, TN) + dot(low, hot, TN)
+    found = dot(jnp.concatenate([high, low], axis=0), jnp.concatenate([hot, hot], axis=0), TN)
     here = sublane_iota(found.shape) == route_ref[1:2, :].astype(jnp.int32)
     out_ref[...] = jnp.sum(jnp.where(here, found, 0.0), axis=0, keepdims=True)
-
-
-def collect(back, routes):
+    result.wait()
+
+
+def collect(back, routes, updated_params):
     return pl.pallas_call(
         collect_kernel,
-        in_specs=[VMEM_SPEC] * 2,
-        out_specs=VMEM_SPEC,
-        out_shape=jax.ShapeDtypeStruct((1, routes.shape[1]), F32),
+        in_specs=[VMEM_SPEC] * 3,
+        out_specs=[VMEM_SPEC, pl.BlockSpec(memory_space=pltpu.HBM)],
+        out_shape=[
+            jax.ShapeDtypeStruct((1, routes.shape[1]), F32),
+            pltpu.HBM(updated_params.shape, F32),
+        ],
+        scratch_shapes=[pltpu.SemaphoreType.DMA],
         compiler_params=vmem(8),
         name="collect",
-    )(back, routes)
+    )(back, routes, pltpu.with_memory_space_constraint(updated_params, pltpu.VMEM))
 
 
 def behind(value, axis):
@@ -454,8 +488,10 @@
     )
     grads = gather(grad, dp)
     updated, send = new_pass(grads, weight, meta, owner_hot, lane_hot, held, row_buf, examples)
-    updated_params, back = members_pass(exchange(send), member_params, member_counts[:, None])
-    total = collect(exchange(back), routes)
+    updated_params, back, routes = members_pass(
+        exchange(send), member_params, member_counts[None], routes
+    )
+    total, updated_params = collect(exchange(back), routes, updated_params)
     return updated[0], updated_params, total[0]
 
 

time: 104 us -> 96.2 us (0.925)
  blocking collectives: 31.6 us -> 67.7 us
  waiting for transfers between devices: 31.6 us -> 0.75 us
  Pallas kernels: 29.8 us -> 22.1 us
  starting transfers between devices: 9.43 us -> 4.5 us
    all_to_all x1 -> x2, blocking collectives: 13 us -> 48.5 us  [exchange(): got = lax.all_to_all(sent, ALL, split_axis=0, concat_axis=0, tiled=True)]
    all_to_all x1 -> x0, waiting for transfers between devices: 31.5 us -> none  [exchange(): got = lax.all_to_all(sent, ALL, split_axis=0, concat_axis=0, tiled=True)]
    all_to_all x1 -> x0, starting transfers between devices: 3.72 us -> none  [exchange(): got = lax.all_to_all(sent, ALL, split_axis=0, concat_axis=0, tiled=True)]
    pallas_call x1, Pallas kernels: 6.82 us -> 3.8 us  [new_pass(): pl.pallas_call(functools.partial(new_kernel, examples=examples), in_specs...]
    pallas_call x3, Pallas kernels: 11.3 us -> 8.53 us  [the longest x1 4.84 us: members_pass(): pl.pallas_call(members_kernel, in_specs=[VMEM_SPEC] * 3 + [pl.BlockSpec(m...]
    pallas_call x1, Pallas kernels: 3.77 us -> 2.55 us  [grad_pass(): pl.pallas_call(grad_kernel, in_specs=[VMEM_SPEC] * 7 + [pl.BlockSpec(memo...]
    ppermute x3, starting transfers between devices: 5.71 us -> 4.5 us  [behind(): lax.ppermute(value, axis, [(i, (i + hop) % size) for i in range(size)])]
  transfers between devices with their start and end apart: 4 -> 3, of which waited for: 1 -> 2; matrix products, arithmetic and copies ran while one was open for 0% -> 0% of each run, Pallas kernels for 4% -> 3%
where the time goes in v2:
time: 96.2 us; the launch traced here: 96 us
  blocking collectives  67.7 us (70%)
  Pallas kernels  22.1 us (23%)
  starting transfers between devices  4.5 us (5%)
    all_to_all x2, blocking collectives, exchange(): got = lax.all_to_all(sent, ALL, split_axis=0, concat_axis=0, tiled=True)  48.5 us
    all_to_all x1, blocking collectives, gather(): return lax.all_to_all(copies, axes, split_axis=0, concat_axis=0, tiled=True)  19.2 us
    pallas_call x1, Pallas kernels, front(): pl.pallas_call(functools.partial(front_kernel, mem_dev=mem_dev, chunks=ch...  7.25 us
    pallas_call x1, Pallas kernels, members_pass(): pl.pallas_call(members_kernel, in_specs=[VMEM_SPEC] * 3 + [pl.BlockSpec(m...  4.84 us
    ppermute x3, starting transfers between devices, behind(): lax.ppermute(value, axis, [(i, (i + hop) % size) for i in range(size)])  4.5 us
    pallas_call x1, Pallas kernels, new_pass(): pl.pallas_call(functools.partial(new_kernel, examples=examples), in_specs...  3.8 us
    pallas_call x1, Pallas kernels, grad_pass(): pl.pallas_call(grad_kernel, in_specs=[VMEM_SPEC] * 7 + [pl.BlockSpec(memo...  2.55 us
    pallas_call x1, Pallas kernels, place(): pl.pallas_call(place_kernel, in_specs=[VMEM_SPEC] * 3, out_specs=[VMEM_SP...  2.48 us
  transfers between devices with their start and end apart: 3, of which 2 were waited for; matrix products, arithmetic and copies ran while one was open for 0% of the time, Pallas kernels for 3%

profile of v2, /device:TPU:1, one launch (start us, length us, event | category | flops | bytes accessed | tf_op | source)
XLA Modules:
  0.0 96.0 jit_solution(1345435355548681568)
XLA Ops:
  0.6 0.0 copy-start
  0.6 0.0 copy-start.1
  0.7 0.0 copy-start.4
  0.7 7.3 %front.1 = (f32[1,5120]{1,0:T(1,128)S(1)}, bf16[4096,2048]{1,0:T(8,128)(2,1)S(1)}, f32[8,1024]{1,0:T(8,128)S(1)}) custom-call(s32[1,1024]{1,0:T(1,128)} %bitcast.25, s32[32,128]{1,0:T(8,128)} %bitcast.24, f32[1,2048]{1,0:T(1,128)} %bitcast.20, bf16[4096,2048]{1,0:T(8,128)(2,1)} %feat_hbm.1), custom_call_target="tpu_custom_call" | custom-call | tf_op jit(solution)/shard_map/front/pallas_call | solution.py:160
  7.9 3.4 %collective-permute-start.2 = (f32[1,5120]{1,0:T(1,128)S(1)}, f32[1,5120]{1,0:T(1,128)S(1)}, u32[]{:S(2)}, u32[]{:S(2)}) collective-permute-start(f32[1,5120]{1,0:T(1,128)S(1)} %get-tuple-element.18.p0), channel_id=1, source_target_pairs={{0,3},{1,0},{2,1},{3,2},{4,7},{5,4},{6,5},{7,6},{8,11},{9,8},{10,9... | collective-permute-start | bytes 61448 | tf_op jit(solution)/shard_map/ppermute | solution.py:444
  11.3 0.5 collective-permute-start.1
  11.8 0.6 collective-permute-start
  12.4 0.0 copy-done
  12.4 0.0 copy-done.1
  12.4 2.5 %place.1 = (f32[4224,128]{1,0:T(8,128)S(1)}, f32[128,128]{1,0:T(8,128)S(1)}) custom-call(f32[8,1024]{1,0:T(8,128)S(1)} %get-tuple-element.20.route_ref.route_hbm, s32[1,4096]{1,0:T(1,128)S(1)} %bitcast.17, f32[1024,256]{1,0:T(8,128)S(1)} %copy-done), custom_call_target="tpu_custom_call" | custom-call | tf_op jit(solution)/shard_map/place/pallas_call | solution.py:210
  14.9 0.0 collective-permute-done.2.p3
  14.9 0.5 collective-permute-done.1.p2
  15.4 0.2 collective-permute-done.p1
  15.7 0.0 copy-done.4
  15.7 0.0 copy-start.2
  15.7 2.5 %grad.1 = (f32[32,16,128]{2,1,0:T(8,128)S(1)}, bf16[128,4096]{1,0:T(8,128)(2,1)S(1)}, bf16[128,4096]{1,0:T(8,128)(2,1)S(1)}) custom-call(f32[1,5120]{1,0:T(1,128)S(1)} %get-tuple-element.18.p0, f32[1,5120]{1,0:T(1,128)S(1)} %collective-permute-done.p1, f32[1,5120]{1,0:T(1,128)S(1)} %collective-permute-done.1.p2, f32[1,5120]{1,0:T(1,128)S(1)} %collective-permute-done.2.p3, ...), custom_call_target="tpu_custom_call" | custom-call | tf_op jit(solution)/shard_map/grad/pallas_call | solution.py:258
  18.2 19.2 %all_to_all.15.grads_ref = f32[32,16,128]{2,1,0:T(8,128)S(1)} all-to-all(f32[32,16,128]{2,1,0:T(8,128)S(1)} %get-tuple-element.22), channel_id=1, replica_groups=mesh['z'=4,'y'=4,'core'=2,'feat'=4] {'z','y','core'}, dimensions={0} | all-to-all | bytes 524288 | tf_op jit(solution)/shard_map/all_to_all | solution.py:450
  37.4 0.0 copy-done.2
  37.4 3.8 %new.1 = (f32[1,2048]{1,0:T(1,128)}, f32[4224,128]{1,0:T(8,128)S(1)}) custom-call(f32[32,16,128]{2,1,0:T(8,128)S(1)} %all_to_all.15.grads_ref, f32[1,2048]{1,0:T(1,128)S(1)} %bitcast.21, f32[128,128]{1,0:T(8,128)S(1)} %get-tuple-element.21.meta_ref, bf16[128,4096]{1,0:T(8,128)(2,1)S(1)} %get-tuple-element.23.owner_ref, ...), custom_call_target="tpu_custom_call", output_to_operand_aliasing={{1}: (6, {})} | custom-call | tf_op jit(solution)/shard_map/new/pallas_call | solution.py:310
  41.2 0.0 copy-start.3
  41.2 0.0 copy-start.5
  41.2 35.5 %all_to_all.16 = f32[128,1,4224]{2,1,0:T(1,128)S(1)} all-to-all(f32[128,1,4224]{2,1,0:T(1,128)S(1)} %bitcast.14), channel_id=1, replica_groups=mesh['z'=4,'y'=4,'core'=2,'feat'=4] {'z','y','core','feat'}, dimensions={0} | all-to-all | bytes 4325376 | tf_op jit(solution)/shard_map/all_to_all | solution.py:455
  76.7 0.0 copy-done.3
  76.7 0.0 copy-done.5
  76.7 4.8 %members.1 = (f32[32,256]{1,0:T(8,128)S(1)}, f32[128,128]{1,0:T(8,128)S(1)}, f32[8,1024]{1,0:T(8,128)S(1)}) custom-call(f32[4224,128]{1,0:T(8,128)S(1)} %bitcast.15, f32[32,256]{1,0:T(8,128)S(1)} %copy-done.3, s32[1,32]{1,0:T(1,128)S(1)} %bitcast.23, f32[8,1024]{1,0:T(8,128)S(1)} %get-tuple-element.20.route_ref.route_hbm), custom_call_target="tpu_custom_call" | custom-call | tf_op jit(solution)/shard_map/members/pallas_call | solution.py:400
  81.6 13.1 %all_to_all.17 = f32[128,1,128]{2,1,0:T(1,128)S(1)} all-to-all(f32[128,1,128]{2,1,0:T(1,128)S(1)} %bitcast.19), channel_id=1, replica_groups=mesh['z'=4,'y'=4,'core'=2,'feat'=4] {'z','y','core','feat'}, dimensions={0} | all-to-all | bytes 131072 | tf_op jit(solution)/shard_map/all_to_all | solution.py:455
  94.6 1.2 %collect.1 = (f32[1,1024]{1,0:T(1,128)}, f32[32,256]{1,0:T(8,128)}) custom-call(f32[128,128]{1,0:T(8,128)S(1)} %bitcast.16, f32[8,1024]{1,0:T(8,128)S(1)} %get-tuple-element.29.route_ref, f32[32,256]{1,0:T(8,128)S(1)} %get-tuple-element.30.params_ref), custom_call_target="tpu_custom_call" | custom-call | tf_op jit(solution)/shard_map/collect/pallas_call | solution.py:427
Async XLA Ops:
  0.6 11.8 %copy-start = (f32[1024,256]{1,0:T(8,128)S(1)}, f32[1024,256]{1,0:T(8,128)}, u32[]{:S(2)}) copy-start(f32[1024,256]{1,0:T(8,128)} %rows_ref.1) | copy-start | bytes 3145732
  0.6 11.8 %copy-start.1 = (s32[4096]{0:T(1024)S(1)}, s32[4096]{0:T(1024)}, u32[]{:S(2)}) copy-start(s32[4096]{0:T(1024)} %param.12) | copy-start | bytes 49156
  0.7 15.0 %copy-start.4 = (f32[4096]{0:T(1024)S(1)}, f32[4096]{0:T(1024)}, u32[]{:S(2)}) copy-start(f32[4096]{0:T(1024)} %param.11) | copy-start | bytes 49156
  7.9 7.0 %collective-permute-start.2 = (f32[1,5120]{1,0:T(1,128)S(1)}, f32[1,5120]{1,0:T(1,128)S(1)}, u32[]{:S(2)}, u32[]{:S(2)}) collective-permute-start(f32[1,5120]{1,0:T(1,128)S(1)} %get-tuple-element.18.p0), channel_id=1, source_target_pairs={{0,3},{1,0},{2,1},{3,2},{4,7},{5,4},{6,5},{7,6},{8,11},{9,8},{10,9... | collective-permute-start | bytes 61448 | tf_op jit(solution)/shard_map/ppermute | solution.py:444
  11.3 4.1 %collective-permute-start.1 = (f32[1,5120]{1,0:T(1,128)S(1)}, f32[1,5120]{1,0:T(1,128)S(1)}, u32[]{:S(2)}, u32[]{:S(2)}) collective-permute-start(f32[1,5120]{1,0:T(1,128)S(1)} %get-tuple-element.18.p0), channel_id=1, source_target_pairs={{0,2},{1,3},{2,0},{3,1},{4,6},{5,7},{6,4},{7,5},{8,10},{9,11},{10,... | collective-permute-start | bytes 61448 | tf_op jit(solution)/shard_map/ppermute | solution.py:444
  11.8 3.8 %collective-permute-start = (f32[1,5120]{1,0:T(1,128)S(1)}, f32[1,5120]{1,0:T(1,128)S(1)}, u32[]{:S(2)}, u32[]{:S(2)}) collective-permute-start(f32[1,5120]{1,0:T(1,128)S(1)} %get-tuple-element.18.p0), channel_id=1, source_target_pairs={{0,1},{1,2},{2,3},{3,0},{4,5},{5,6},{6,7},{7,4},{8,9},{9,10},{10,1... | collective-permute-start | bytes 61448 | tf_op jit(solution)/shard_map/ppermute | solution.py:444
  15.7 21.7 %copy-start.2 = (f32[2048]{0:T(1024)S(1)}, f32[2048]{0:T(1024)}, u32[]{:S(2)}) copy-start(f32[2048]{0:T(1024)} %param.10) | copy-start | bytes 24580
  41.2 35.5 %copy-start.3 = (f32[32,256]{1,0:T(8,128)S(1)}, f32[32,256]{1,0:T(8,128)}, u32[]{:S(2)}) copy-start(f32[32,256]{1,0:T(8,128)} %params_ref.1) | copy-start | bytes 98308
  41.2 35.5 %copy-start.5 = (s32[32]{0:T(128)S(1)}, s32[32]{0:T(128)}, u32[]{:S(2)}) copy-start(s32[32]{0:T(128)} %param.15) | copy-start | bytes 388

commit v3 on v2

--- a/solution.py
+++ b/solution.py
@@ -148,7 +148,8 @@
     start = 0
     for copy, size in zip(copies, chunks):
         copy.wait()
-        packet_ref[:, start : start + size] = margin_chunk(weight, feat_ref, start, size)
+        for first in range(start, start + size, 512):
+            packet_ref[:, first : first + 512] = margin_chunk(weight, feat_ref, first, 512)
         start += size
 
 
@@ -328,14 +329,37 @@
 
 
 def members_kernel(
-    recv_ref, params_ref, counts_ref, route_hbm, out_ref, back_ref, route_ref, high_ref, low_ref, sem
+    recv_ref,
+    params_ref,
+    counts_ref,
+    route_hbm,
+    out_ref,
+    back_ref,
+    route_ref,
+    high_ref,
+    low_ref,
+    across_high_ref,
+    across_low_ref,
+    sem,
 ):
     keep = pltpu.make_async_copy(route_hbm, route_ref, sem)
     keep.start()
-    for k in range(CAPACITY):
-        rows = jnp.concatenate([recv_ref[per_owner(LEFT + k), :], recv_ref[per_owner(RIGHT + k), :]], axis=1)
-        here = pl.ds(k * LANES, LANES)
-        high_ref[here, :], low_ref[here, :] = split(rows)
+    old = params_ref[...]
+    old_scores = []
+    for k in range(0, CAPACITY, 2):
+        rows = jnp.concatenate(
+            [
+                jnp.concatenate([recv_ref[per_owner(LEFT + i), :], recv_ref[per_owner(RIGHT + i), :]], axis=1)
+                for i in (k, k + 1)
+            ],
+            axis=0,
+        )
+        here = pl.ds(k * LANES, 2 * LANES)
+        high, low = split(rows)
+        high_ref[here, :], low_ref[here, :] = high, low
+        high, low = split(rows.T)
+        across_high_ref[:, here], across_low_ref[:, here] = high, low
+        old_scores.append(dot_split(old, high, low, NN))
     side = recv_ref[per_owner(SIDE), :].T
     groups = lax.axis_size("feat")
     lane = lane_iota((CAPACITY, LANES))
@@ -357,11 +381,11 @@
         return jnp.sum(jnp.where(mask, value, 0.0), axis=0, keepdims=True)
 
     high, low = high_ref[...], low_ref[...]
-    old = params_ref[...]
+    across_high, across_low = across_high_ref[...], across_low_ref[...]
     diagonal = sublane_iota((members, members)) == lane_iota((members, members))
     scales = jnp.broadcast_to(1.0 / (counts_ref[...].astype(F32) + 1.0), (members, members))
     scaling = jnp.sum(jnp.where(diagonal, scales, 0.0), axis=1, keepdims=True)
-    margin = offset + own(dot_split(old, high, low, NT))
+    margin = offset + own(jnp.concatenate(old_scores, axis=1))
     probability = jax.nn.sigmoid(margin)
     weight = probability * (1.0 - probability)
     errors = jnp.where(mask, label - probability, 0.0)
@@ -370,7 +394,7 @@
     delta = jnp.zeros_like(remains)
     norm_now = jnp.sum(remains * remains, axis=1, keepdims=True)
     for step in range(CG_STEPS):
-        along = jnp.where(mask, dot_split(direction, high, None if step == 2 else low, NT), 0.0)
+        along = jnp.where(mask, dot_split(direction, across_high, None if step == 2 else across_low, NN), 0.0)
         weighted = along * weight
         curve = scaling * jnp.sum(weighted * along, axis=1, keepdims=True) + RIDGE_MEMBER * jnp.sum(
             direction * direction, axis=1, keepdims=True
@@ -396,7 +420,8 @@
 
 def members_pass(recv, member_params, counts, routes):
     members, width = member_params.shape
-    held = pltpu.VMEM((LANES * CAPACITY, width), BF16)
+    slots = LANES * CAPACITY
+    held, across = pltpu.VMEM((slots, width), BF16), pltpu.VMEM((width, slots), BF16)
     return pl.pallas_call(
         members_kernel,
         in_specs=[VMEM_SPEC] * 3 + [pl.BlockSpec(memory_space=pl.ANY)],
@@ -406,33 +431,33 @@
             jax.ShapeDtypeStruct((LANES, LANES), F32),
             pltpu.VMEM(routes.shape, F32),
         ],
-        scratch_shapes=[held, held, pltpu.SemaphoreType.DMA],
+        scratch_shapes=[held, held, across, across, pltpu.SemaphoreType.DMA],
         compiler_params=vmem(16),
         name="members",
     )(recv, member_params, counts, routes)
 
 
-def collect_kernel(back_ref, route_ref, params_ref, out_ref, params_hbm, sem):
-    result = pltpu.make_async_copy(params_ref, params_hbm, sem)
+def collect_kernel(back_ref, route_ref, params_ref, out_hbm, params_hbm, out_ref, sems):
+    result = pltpu.make_async_copy(params_ref, params_hbm, sems.at[0])
     result.start()
     high, low = split(back_ref[:, :CAPACITY])
     hot = hot_rows(LANES, route_ref[0:1, :].astype(jnp.int32))
     found = dot(jnp.concatenate([high, low], axis=0), jnp.concatenate([hot, hot], axis=0), TN)
     here = sublane_iota(found.shape) == route_ref[1:2, :].astype(jnp.int32)
     out_ref[...] = jnp.sum(jnp.where(here, found, 0.0), axis=0, keepdims=True)
+    out = pltpu.make_async_copy(out_ref, out_hbm, sems.at[1])
+    out.start()
     result.wait()
+    out.wait()
 
 
 def collect(back, routes, updated_params):
     return pl.pallas_call(
         collect_kernel,
         in_specs=[VMEM_SPEC] * 3,
-        out_specs=[VMEM_SPEC, pl.BlockSpec(memory_space=pltpu.HBM)],
-        out_shape=[
-            jax.ShapeDtypeStruct((1, routes.shape[1]), F32),
-            pltpu.HBM(updated_params.shape, F32),
-        ],
-        scratch_shapes=[pltpu.SemaphoreType.DMA],
+        out_specs=[pl.BlockSpec(memory_space=pltpu.HBM)] * 2,
+        out_shape=[pltpu.HBM((1, routes.shape[1]), F32), pltpu.HBM(updated_params.shape, F32)],
+        scratch_shapes=[pltpu.VMEM((1, routes.shape[1]), F32), pltpu.SemaphoreType.DMA((2,))],
         compiler_params=vmem(8),
         name="collect",
     )(back, routes, pltpu.with_memory_space_constraint(updated_params, pltpu.VMEM))

time: 96.2 us -> 95.3 us (level)
  no operation moved by 1% of the time
where the time goes in v3:
time: 95.3 us; the launch traced here: 95.1 us
  blocking collectives  67.7 us (71%)
  Pallas kernels  21.2 us (22%)
  starting transfers between devices  4.5 us (5%)
    all_to_all x2, blocking collectives, exchange(): got = lax.all_to_all(sent, ALL, split_axis=0, concat_axis=0, tiled=True)  48.5 us
    all_to_all x1, blocking collectives, gather(): return lax.all_to_all(copies, axes, split_axis=0, concat_axis=0, tiled=True)  19.2 us
    pallas_call x1, Pallas kernels, front(): pl.pallas_call(functools.partial(front_kernel, mem_dev=mem_dev, chunks=ch...  7.24 us
    ppermute x3, starting transfers between devices, behind(): lax.ppermute(value, axis, [(i, (i + hop) % size) for i in range(size)])  4.5 us
    pallas_call x1, Pallas kernels, members_pass(): pl.pallas_call(members_kernel, in_specs=[VMEM_SPEC] * 3 + [pl.BlockSpec(m...  4.36 us
    pallas_call x1, Pallas kernels, new_pass(): pl.pallas_call(functools.partial(new_kernel, examples=examples), in_specs...  3.8 us
    pallas_call x1, Pallas kernels, grad_pass(): pl.pallas_call(grad_kernel, in_specs=[VMEM_SPEC] * 7 + [pl.BlockSpec(memo...  2.55 us
    pallas_call x1, Pallas kernels, place(): pl.pallas_call(place_kernel, in_specs=[VMEM_SPEC] * 3, out_specs=[VMEM_SP...  2.47 us
  transfers between devices with their start and end apart: 3, of which 2 were waited for; matrix products, arithmetic and copies ran while one was open for 0% of the time, Pallas kernels for 3%

profile of v3, /device:TPU:1, one launch (start us, length us, event | category | flops | bytes accessed | tf_op | source)
XLA Modules:
  0.0 95.1 jit_solution(15491348960503849029)
XLA Ops:
  0.6 0.0 copy-start
  0.6 0.0 copy-start.1
  0.7 0.0 copy-start.4
  0.7 7.2 %front.1 = (f32[1,5120]{1,0:T(1,128)S(1)}, bf16[4096,2048]{1,0:T(8,128)(2,1)S(1)}, f32[8,1024]{1,0:T(8,128)S(1)}) custom-call(s32[1,1024]{1,0:T(1,128)} %bitcast.25, s32[32,128]{1,0:T(8,128)} %bitcast.24, f32[1,2048]{1,0:T(1,128)} %bitcast.20, bf16[4096,2048]{1,0:T(8,128)(2,1)} %feat_hbm.1), custom_call_target="tpu_custom_call" | custom-call | tf_op jit(solution)/shard_map/front/pallas_call | solution.py:161
  7.9 3.4 %collective-permute-start.2 = (f32[1,5120]{1,0:T(1,128)S(1)}, f32[1,5120]{1,0:T(1,128)S(1)}, u32[]{:S(2)}, u32[]{:S(2)}) collective-permute-start(f32[1,5120]{1,0:T(1,128)S(1)} %get-tuple-element.18.p0), channel_id=1, source_target_pairs={{0,3},{1,0},{2,1},{3,2},{4,7},{5,4},{6,5},{7,6},{8,11},{9,8},{10,9... | collective-permute-start | bytes 61448 | tf_op jit(solution)/shard_map/ppermute | solution.py:469
  11.3 0.5 collective-permute-start.1
  11.8 0.6 collective-permute-start
  12.4 0.0 copy-done
  12.4 0.0 copy-done.1
  12.4 2.5 %place.1 = (f32[4224,128]{1,0:T(8,128)S(1)}, f32[128,128]{1,0:T(8,128)S(1)}) custom-call(f32[8,1024]{1,0:T(8,128)S(1)} %get-tuple-element.20.route_ref.route_hbm, s32[1,4096]{1,0:T(1,128)S(1)} %bitcast.17, f32[1024,256]{1,0:T(8,128)S(1)} %copy-done), custom_call_target="tpu_custom_call" | custom-call | tf_op jit(solution)/shard_map/place/pallas_call | solution.py:211
  14.9 0.0 collective-permute-done.2.p3
  14.9 0.5 collective-permute-done.1.p2
  15.4 0.2 collective-permute-done.p1
  15.7 0.0 copy-done.4
  15.7 0.0 copy-start.2
  15.7 2.5 %grad.1 = (f32[32,16,128]{2,1,0:T(8,128)S(1)}, bf16[128,4096]{1,0:T(8,128)(2,1)S(1)}, bf16[128,4096]{1,0:T(8,128)(2,1)S(1)}) custom-call(f32[1,5120]{1,0:T(1,128)S(1)} %get-tuple-element.18.p0, f32[1,5120]{1,0:T(1,128)S(1)} %collective-permute-done.p1, f32[1,5120]{1,0:T(1,128)S(1)} %collective-permute-done.1.p2, f32[1,5120]{1,0:T(1,128)S(1)} %collective-permute-done.2.p3, ...), custom_call_target="tpu_custom_call" | custom-call | tf_op jit(solution)/shard_map/grad/pallas_call | solution.py:259
  18.2 19.2 %all_to_all.15.grads_ref = f32[32,16,128]{2,1,0:T(8,128)S(1)} all-to-all(f32[32,16,128]{2,1,0:T(8,128)S(1)} %get-tuple-element.22), channel_id=1, replica_groups=mesh['z'=4,'y'=4,'core'=2,'feat'=4] {'z','y','core'}, dimensions={0} | all-to-all | bytes 524288 | tf_op jit(solution)/shard_map/all_to_all | solution.py:475
  37.4 0.0 copy-done.2
  37.4 3.8 %new.1 = (f32[1,2048]{1,0:T(1,128)}, f32[4224,128]{1,0:T(8,128)S(1)}) custom-call(f32[32,16,128]{2,1,0:T(8,128)S(1)} %all_to_all.15.grads_ref, f32[1,2048]{1,0:T(1,128)S(1)} %bitcast.21, f32[128,128]{1,0:T(8,128)S(1)} %get-tuple-element.21.meta_ref, bf16[128,4096]{1,0:T(8,128)(2,1)S(1)} %get-tuple-element.23.owner_ref, ...), custom_call_target="tpu_custom_call", output_to_operand_aliasing={{1}: (6, {})} | custom-call | tf_op jit(solution)/shard_map/new/pallas_call | solution.py:311
  41.2 0.0 copy-start.3
  41.2 0.0 copy-start.5
  41.2 35.5 %all_to_all.16 = f32[128,1,4224]{2,1,0:T(1,128)S(1)} all-to-all(f32[128,1,4224]{2,1,0:T(1,128)S(1)} %bitcast.14), channel_id=1, replica_groups=mesh['z'=4,'y'=4,'core'=2,'feat'=4] {'z','y','core','feat'}, dimensions={0} | all-to-all | bytes 4325376 | tf_op jit(solution)/shard_map/all_to_all | solution.py:480
  76.7 0.0 copy-done.3
  76.7 0.0 copy-done.5
  76.7 4.4 %members.1 = (f32[32,256]{1,0:T(8,128)S(1)}, f32[128,128]{1,0:T(8,128)S(1)}, f32[8,1024]{1,0:T(8,128)S(1)}) custom-call(f32[4224,128]{1,0:T(8,128)S(1)} %bitcast.15, f32[32,256]{1,0:T(8,128)S(1)} %copy-done.3, s32[1,32]{1,0:T(1,128)S(1)} %bitcast.23, f32[8,1024]{1,0:T(8,128)S(1)} %get-tuple-element.20.route_ref.route_hbm), custom_call_target="tpu_custom_call" | custom-call | tf_op jit(solution)/shard_map/members/pallas_call | solution.py:425
  81.1 13.0 %all_to_all.17 = f32[128,1,128]{2,1,0:T(1,128)S(1)} all-to-all(f32[128,1,128]{2,1,0:T(1,128)S(1)} %bitcast.19), channel_id=1, replica_groups=mesh['z'=4,'y'=4,'core'=2,'feat'=4] {'z','y','core','feat'}, dimensions={0} | all-to-all | bytes 131072 | tf_op jit(solution)/shard_map/all_to_all | solution.py:480
  94.1 0.8 collect.1
Async XLA Ops:
  0.6 11.8 %copy-start = (f32[1024,256]{1,0:T(8,128)S(1)}, f32[1024,256]{1,0:T(8,128)}, u32[]{:S(2)}) copy-start(f32[1024,256]{1,0:T(8,128)} %rows_ref.1) | copy-start | bytes 3145732
  0.6 11.8 %copy-start.1 = (s32[4096]{0:T(1024)S(1)}, s32[4096]{0:T(1024)}, u32[]{:S(2)}) copy-start(s32[4096]{0:T(1024)} %param.12) | copy-start | bytes 49156
  0.7 15.0 %copy-start.4 = (f32[4096]{0:T(1024)S(1)}, f32[4096]{0:T(1024)}, u32[]{:S(2)}) copy-start(f32[4096]{0:T(1024)} %param.11) | copy-start | bytes 49156
  7.9 7.0 %collective-permute-start.2 = (f32[1,5120]{1,0:T(1,128)S(1)}, f32[1,5120]{1,0:T(1,128)S(1)}, u32[]{:S(2)}, u32[]{:S(2)}) collective-permute-start(f32[1,5120]{1,0:T(1,128)S(1)} %get-tuple-element.18.p0), channel_id=1, source_target_pairs={{0,3},{1,0},{2,1},{3,2},{4,7},{5,4},{6,5},{7,6},{8,11},{9,8},{10,9... | collective-permute-start | bytes 61448 | tf_op jit(solution)/shard_map/ppermute | solution.py:469
  11.3 4.1 %collective-permute-start.1 = (f32[1,5120]{1,0:T(1,128)S(1)}, f32[1,5120]{1,0:T(1,128)S(1)}, u32[]{:S(2)}, u32[]{:S(2)}) collective-permute-start(f32[1,5120]{1,0:T(1,128)S(1)} %get-tuple-element.18.p0), channel_id=1, source_target_pairs={{0,2},{1,3},{2,0},{3,1},{4,6},{5,7},{6,4},{7,5},{8,10},{9,11},{10,... | collective-permute-start | bytes 61448 | tf_op jit(solution)/shard_map/ppermute | solution.py:469
  11.8 3.8 %collective-permute-start = (f32[1,5120]{1,0:T(1,128)S(1)}, f32[1,5120]{1,0:T(1,128)S(1)}, u32[]{:S(2)}, u32[]{:S(2)}) collective-permute-start(f32[1,5120]{1,0:T(1,128)S(1)} %get-tuple-element.18.p0), channel_id=1, source_target_pairs={{0,1},{1,2},{2,3},{3,0},{4,5},{5,6},{6,7},{7,4},{8,9},{9,10},{10,1... | collective-permute-start | bytes 61448 | tf_op jit(solution)/shard_map/ppermute | solution.py:469
  15.7 21.7 %copy-start.2 = (f32[2048]{0:T(1024)S(1)}, f32[2048]{0:T(1024)}, u32[]{:S(2)}) copy-start(f32[2048]{0:T(1024)} %param.10) | copy-start | bytes 24580
  41.2 35.5 %copy-start.3 = (f32[32,256]{1,0:T(8,128)S(1)}, f32[32,256]{1,0:T(8,128)}, u32[]{:S(2)}) copy-start(f32[32,256]{1,0:T(8,128)} %params_ref.1) | copy-start | bytes 98308
  41.2 35.5 %copy-start.5 = (s32[32]{0:T(128)S(1)}, s32[32]{0:T(128)}, u32[]{:S(2)}) copy-start(s32[32]{0:T(128)} %param.15) | copy-start | bytes 388

commit v4 on v3

--- a/solution.py
+++ b/solution.py
@@ -19,6 +19,7 @@
 CAPACITY = 16
 LEFT, RIGHT, SIDE, MESSAGE = 0, CAPACITY, 2 * CAPACITY, 2 * CAPACITY + 1
 ALL = ("z", "y", "core", "feat")
+BACK = ("core", "z", "y", "feat")
 NN = (((1,), (0,)), ((), ()))
 NT = (((1,), (1,)), ((), ()))
 TN = (((0,), (0,)), ((), ()))
@@ -414,7 +415,12 @@
         + [jnp.zeros((LANES - CAPACITY, LANES), F32)],
         axis=0,
     )
-    back_ref[...] = table.T
+    by_source = table.T
+    cores, chip = lax.axis_size("core"), lax.axis_size("feat")
+    for number in range(LANES // chip):
+        core, place = number % cores, number // cores
+        start = core * (LANES // cores) + place * chip
+        back_ref[start : start + chip, :] = by_source[number * chip : (number + 1) * chip]
     keep.wait()
 
 
@@ -441,7 +447,10 @@
     result = pltpu.make_async_copy(params_ref, params_hbm, sems.at[0])
     result.start()
     high, low = split(back_ref[:, :CAPACITY])
-    hot = hot_rows(LANES, route_ref[0:1, :].astype(jnp.int32))
+    owner = route_ref[0:1, :].astype(jnp.int32)
+    cores, chip = lax.axis_size("core"), lax.axis_size("feat")
+    core, place = owner // chip % cores, owner // (chip * cores)
+    hot = hot_rows(LANES, core * (LANES // cores) + place * chip + owner % chip)
     found = dot(jnp.concatenate([high, low], axis=0), jnp.concatenate([hot, hot], axis=0), TN)
     here = sublane_iota(found.shape) == route_ref[1:2, :].astype(jnp.int32)
     out_ref[...] = jnp.sum(jnp.where(here, found, 0.0), axis=0, keepdims=True)
@@ -475,9 +484,9 @@
     return lax.all_to_all(copies, axes, split_axis=0, concat_axis=0, tiled=True)
 
 
-def exchange(table):
+def exchange(table, axes):
     sent = table.reshape(LANES, 1, -1)
-    got = lax.all_to_all(sent, ALL, split_axis=0, concat_axis=0, tiled=True)
+    got = lax.all_to_all(sent, axes, split_axis=0, concat_axis=0, tiled=True)
     return got.reshape(table.shape)
 
 
@@ -507,16 +516,16 @@
     )
     packets = behind(packet, "feat")
     row_buf, meta = place(routes, label_row, member_features)
-    dp = ("z", "y", "core")
+    dp = ("core", "z", "y")
     grad, owner_hot, lane_hot = grad_pass(
         packets, prior_offset[None], label_row, held, meta, lax.axis_size(dp)
     )
     grads = gather(grad, dp)
     updated, send = new_pass(grads, weight, meta, owner_hot, lane_hot, held, row_buf, examples)
     updated_params, back, routes = members_pass(
-        exchange(send), member_params, member_counts[None], routes
-    )
-    total, updated_params = collect(exchange(back), routes, updated_params)
+        exchange(send, ALL), member_params, member_counts[None], routes
+    )
+    total, updated_params = collect(exchange(back, BACK), routes, updated_params)
     return updated[0], updated_params, total[0]
 
 

time: 95.3 us -> 95.1 us (level)
  no operation moved by 1% of the time
where the time goes in v4:
time: 95.1 us; the launch traced here: 94.9 us
  blocking collectives  67.5 us (71%)
  Pallas kernels  21.3 us (22%)
  starting transfers between devices  4.5 us (5%)
    all_to_all x2, blocking collectives, exchange(): got = lax.all_to_all(sent, axes, split_axis=0, concat_axis=0, tiled=True)  48.9 us
    all_to_all x1, blocking collectives, gather(): return lax.all_to_all(copies, axes, split_axis=0, concat_axis=0, tiled=True)  18.6 us
    pallas_call x1, Pallas kernels, front(): pl.pallas_call(functools.partial(front_kernel, mem_dev=mem_dev, chunks=ch...  7.24 us
    ppermute x3, starting transfers between devices, behind(): lax.ppermute(value, axis, [(i, (i + hop) % size) for i in range(size)])  4.5 us
    pallas_call x1, Pallas kernels, members_pass(): pl.pallas_call(members_kernel, in_specs=[VMEM_SPEC] * 3 + [pl.BlockSpec(m...  4.36 us
    pallas_call x1, Pallas kernels, new_pass(): pl.pallas_call(functools.partial(new_kernel, examples=examples), in_specs...  3.8 us
    pallas_call x1, Pallas kernels, grad_pass(): pl.pallas_call(grad_kernel, in_specs=[VMEM_SPEC] * 7 + [pl.BlockSpec(memo...  2.55 us
    pallas_call x1, Pallas kernels, place(): pl.pallas_call(place_kernel, in_specs=[VMEM_SPEC] * 3, out_specs=[VMEM_SP...  2.47 us
  transfers between devices with their start and end apart: 3, of which 2 were waited for; matrix products, arithmetic and copies ran while one was open for 0% of the time, Pallas kernels for 3%

profile of v4, /device:TPU:1, one launch (start us, length us, event | category | flops | bytes accessed | tf_op | source)
XLA Modules:
  0.0 94.9 jit_solution(2329781500636155507)
XLA Ops:
  0.6 0.0 copy-start
  0.6 0.0 copy-start.1
  0.7 0.0 copy-start.4
  0.7 7.2 %front.1 = (f32[1,5120]{1,0:T(1,128)S(1)}, bf16[4096,2048]{1,0:T(8,128)(2,1)S(1)}, f32[8,1024]{1,0:T(8,128)S(1)}) custom-call(s32[1,1024]{1,0:T(1,128)} %bitcast.25, s32[32,128]{1,0:T(8,128)} %bitcast.24, f32[1,2048]{1,0:T(1,128)} %bitcast.20, bf16[4096,2048]{1,0:T(8,128)(2,1)} %feat_hbm.1), custom_call_target="tpu_custom_call" | custom-call | tf_op jit(solution)/shard_map/front/pallas_call | solution.py:162
  7.9 3.4 %collective-permute-start.2 = (f32[1,5120]{1,0:T(1,128)S(1)}, f32[1,5120]{1,0:T(1,128)S(1)}, u32[]{:S(2)}, u32[]{:S(2)}) collective-permute-start(f32[1,5120]{1,0:T(1,128)S(1)} %get-tuple-element.18.p0), channel_id=1, source_target_pairs={{0,3},{1,0},{2,1},{3,2},{4,7},{5,4},{6,5},{7,6},{8,11},{9,8},{10,9... | collective-permute-start | bytes 61448 | tf_op jit(solution)/shard_map/ppermute | solution.py:478
  11.3 0.5 collective-permute-start.1
  11.8 0.6 collective-permute-start
  12.4 0.0 copy-done
  12.4 0.0 copy-done.1
  12.4 2.5 %place.1 = (f32[4224,128]{1,0:T(8,128)S(1)}, f32[128,128]{1,0:T(8,128)S(1)}) custom-call(f32[8,1024]{1,0:T(8,128)S(1)} %get-tuple-element.20.route_ref.route_hbm, s32[1,4096]{1,0:T(1,128)S(1)} %bitcast.17, f32[1024,256]{1,0:T(8,128)S(1)} %copy-done), custom_call_target="tpu_custom_call" | custom-call | tf_op jit(solution)/shard_map/place/pallas_call | solution.py:212
  14.9 0.0 collective-permute-done.2.p3
  14.9 0.5 collective-permute-done.1.p2
  15.4 0.2 collective-permute-done.p1
  15.7 0.0 copy-done.4
  15.7 0.0 copy-start.2
  15.7 2.5 %grad.1 = (f32[32,16,128]{2,1,0:T(8,128)S(1)}, bf16[128,4096]{1,0:T(8,128)(2,1)S(1)}, bf16[128,4096]{1,0:T(8,128)(2,1)S(1)}) custom-call(f32[1,5120]{1,0:T(1,128)S(1)} %get-tuple-element.18.p0, f32[1,5120]{1,0:T(1,128)S(1)} %collective-permute-done.p1, f32[1,5120]{1,0:T(1,128)S(1)} %collective-permute-done.1.p2, f32[1,5120]{1,0:T(1,128)S(1)} %collective-permute-done.2.p3, ...), custom_call_target="tpu_custom_call" | custom-call | tf_op jit(solution)/shard_map/grad/pallas_call | solution.py:260
  18.2 18.6 %all_to_all.15.grads_ref = f32[32,16,128]{2,1,0:T(8,128)S(1)} all-to-all(f32[32,16,128]{2,1,0:T(8,128)S(1)} %get-tuple-element.22), channel_id=1, replica_groups=mesh['z'=4,'y'=4,'core'=2,'feat'=4] {'core','z','y'}, dimensions={0} | all-to-all | bytes 524288 | tf_op jit(solution)/shard_map/all_to_all | solution.py:484
  36.8 0.0 copy-done.2
  36.8 3.8 %new.1 = (f32[1,2048]{1,0:T(1,128)}, f32[4224,128]{1,0:T(8,128)S(1)}) custom-call(f32[32,16,128]{2,1,0:T(8,128)S(1)} %all_to_all.15.grads_ref, f32[1,2048]{1,0:T(1,128)S(1)} %bitcast.21, f32[128,128]{1,0:T(8,128)S(1)} %get-tuple-element.21.meta_ref, bf16[128,4096]{1,0:T(8,128)(2,1)S(1)} %get-tuple-element.23.owner_ref, ...), custom_call_target="tpu_custom_call", output_to_operand_aliasing={{1}: (6, {})} | custom-call | tf_op jit(solution)/shard_map/new/pallas_call | solution.py:312
  40.6 0.0 copy-start.3
  40.6 0.0 copy-start.5
  40.6 36.0 %all_to_all.16 = f32[128,1,4224]{2,1,0:T(1,128)S(1)} all-to-all(f32[128,1,4224]{2,1,0:T(1,128)S(1)} %bitcast.14), channel_id=1, replica_groups=mesh['z'=4,'y'=4,'core'=2,'feat'=4] {'z','y','core','feat'}, dimensions={0} | all-to-all | bytes 4325376 | tf_op jit(solution)/shard_map/all_to_all | solution.py:489
  76.7 0.0 copy-done.3
  76.7 0.0 copy-done.5
  76.7 4.4 %members.1 = (f32[32,256]{1,0:T(8,128)S(1)}, f32[128,128]{1,0:T(8,128)S(1)}, f32[8,1024]{1,0:T(8,128)S(1)}) custom-call(f32[4224,128]{1,0:T(8,128)S(1)} %bitcast.15, f32[32,256]{1,0:T(8,128)S(1)} %copy-done.3, s32[1,32]{1,0:T(1,128)S(1)} %bitcast.23, f32[8,1024]{1,0:T(8,128)S(1)} %get-tuple-element.20.route_ref.route_hbm), custom_call_target="tpu_custom_call" | custom-call | tf_op jit(solution)/shard_map/members/pallas_call | solution.py:431
  81.0 12.9 %all_to_all.17 = f32[128,1,128]{2,1,0:T(1,128)S(1)} all-to-all(f32[128,1,128]{2,1,0:T(1,128)S(1)} %bitcast.19), channel_id=1, replica_groups=mesh['z'=4,'y'=4,'core'=2,'feat'=4] {'core','z','y','feat'}, dimensions={0} | all-to-all | bytes 131072 | tf_op jit(solution)/shard_map/all_to_all | solution.py:489
  93.9 0.8 collect.1
Async XLA Ops:
  0.6 11.8 %copy-start = (f32[1024,256]{1,0:T(8,128)S(1)}, f32[1024,256]{1,0:T(8,128)}, u32[]{:S(2)}) copy-start(f32[1024,256]{1,0:T(8,128)} %rows_ref.1) | copy-start | bytes 3145732
  0.6 11.8 %copy-start.1 = (s32[4096]{0:T(1024)S(1)}, s32[4096]{0:T(1024)}, u32[]{:S(2)}) copy-start(s32[4096]{0:T(1024)} %param.12) | copy-start | bytes 49156
  0.7 15.0 %copy-start.4 = (f32[4096]{0:T(1024)S(1)}, f32[4096]{0:T(1024)}, u32[]{:S(2)}) copy-start(f32[4096]{0:T(1024)} %param.11) | copy-start | bytes 49156
  7.9 7.0 %collective-permute-start.2 = (f32[1,5120]{1,0:T(1,128)S(1)}, f32[1,5120]{1,0:T(1,128)S(1)}, u32[]{:S(2)}, u32[]{:S(2)}) collective-permute-start(f32[1,5120]{1,0:T(1,128)S(1)} %get-tuple-element.18.p0), channel_id=1, source_target_pairs={{0,3},{1,0},{2,1},{3,2},{4,7},{5,4},{6,5},{7,6},{8,11},{9,8},{10,9... | collective-permute-start | bytes 61448 | tf_op jit(solution)/shard_map/ppermute | solution.py:478
  11.3 4.1 %collective-permute-start.1 = (f32[1,5120]{1,0:T(1,128)S(1)}, f32[1,5120]{1,0:T(1,128)S(1)}, u32[]{:S(2)}, u32[]{:S(2)}) collective-permute-start(f32[1,5120]{1,0:T(1,128)S(1)} %get-tuple-element.18.p0), channel_id=1, source_target_pairs={{0,2},{1,3},{2,0},{3,1},{4,6},{5,7},{6,4},{7,5},{8,10},{9,11},{10,... | collective-permute-start | bytes 61448 | tf_op jit(solution)/shard_map/ppermute | solution.py:478
  11.8 3.8 %collective-permute-start = (f32[1,5120]{1,0:T(1,128)S(1)}, f32[1,5120]{1,0:T(1,128)S(1)}, u32[]{:S(2)}, u32[]{:S(2)}) collective-permute-start(f32[1,5120]{1,0:T(1,128)S(1)} %get-tuple-element.18.p0), channel_id=1, source_target_pairs={{0,1},{1,2},{2,3},{3,0},{4,5},{5,6},{6,7},{7,4},{8,9},{9,10},{10,1... | collective-permute-start | bytes 61448 | tf_op jit(solution)/shard_map/ppermute | solution.py:478
  15.7 21.1 %copy-start.2 = (f32[2048]{0:T(1024)S(1)}, f32[2048]{0:T(1024)}, u32[]{:S(2)}) copy-start(f32[2048]{0:T(1024)} %param.10) | copy-start | bytes 24580
  40.6 36.1 %copy-start.3 = (f32[32,256]{1,0:T(8,128)S(1)}, f32[32,256]{1,0:T(8,128)}, u32[]{:S(2)}) copy-start(f32[32,256]{1,0:T(8,128)} %params_ref.1) | copy-start | bytes 98308
  40.6 36.0 %copy-start.5 = (s32[32]{0:T(128)S(1)}, s32[32]{0:T(128)}, u32[]{:S(2)}) copy-start(s32[32]{0:T(128)} %param.15) | copy-start | bytes 388

commit v5 on v4

--- a/solution.py
+++ b/solution.py
@@ -474,10 +474,9 @@
 
 def behind(value, axis):
     size = lax.axis_size(axis)
-    return [value] + [
-        lax.ppermute(value, axis, [(i, (i + hop) % size) for i in range(size)])
-        for hop in range(1, size)
-    ]
+    order = sorted(range(1, size), key=lambda hop: min(hop, size - hop))
+    got = {hop: lax.ppermute(value, axis, [(i, (i + hop) % size) for i in range(size)]) for hop in order}
+    return [value] + [got[hop] for hop in range(1, size)]
 
 
 def gather(copies, axes):

time: 95.1 us -> 95.1 us (level)
  no operation moved by 1% of the time
where the time goes in v5:
time: 95.1 us; the launch traced here: 94.9 us
  blocking collectives  67.5 us (71%)
  Pallas kernels  21.3 us (22%)
  starting transfers between devices  4.5 us (5%)
    all_to_all x2, blocking collectives, exchange(): got = lax.all_to_all(sent, axes, split_axis=0, concat_axis=0, tiled=True)  48.9 us
    all_to_all x1, blocking collectives, gather(): return lax.all_to_all(copies, axes, split_axis=0, concat_axis=0, tiled=True)  18.6 us
    pallas_call x1, Pallas kernels, front(): pl.pallas_call(functools.partial(front_kernel, mem_dev=mem_dev, chunks=ch...  7.24 us
    ppermute x3, starting transfers between devices, behind(): lax.ppermute(value, axis, [(i, (i + hop) % size) for i in range(size)])  4.5 us
    pallas_call x1, Pallas kernels, members_pass(): pl.pallas_call(members_kernel, in_specs=[VMEM_SPEC] * 3 + [pl.BlockSpec(m...  4.36 us
    pallas_call x1, Pallas kernels, new_pass(): pl.pallas_call(functools.partial(new_kernel, examples=examples), in_specs...  3.8 us
    pallas_call x1, Pallas kernels, grad_pass(): pl.pallas_call(grad_kernel, in_specs=[VMEM_SPEC] * 7 + [pl.BlockSpec(memo...  2.55 us
    pallas_call x1, Pallas kernels, place(): pl.pallas_call(place_kernel, in_specs=[VMEM_SPEC] * 3, out_specs=[VMEM_SP...  2.47 us
  transfers between devices with their start and end apart: 3, of which 2 were waited for; matrix products, arithmetic and copies ran while one was open for 0% of the time, Pallas kernels for 3%

profile of v5, /device:TPU:1, one launch (start us, length us, event | category | flops | bytes accessed | tf_op | source)
XLA Modules:
  0.0 94.9 jit_solution(2329781500636155507)
XLA Ops:
  0.6 0.0 copy-start
  0.6 0.0 copy-start.1
  0.7 0.0 copy-start.4
  0.7 7.2 %front.1 = (f32[1,5120]{1,0:T(1,128)S(1)}, bf16[4096,2048]{1,0:T(8,128)(2,1)S(1)}, f32[8,1024]{1,0:T(8,128)S(1)}) custom-call(s32[1,1024]{1,0:T(1,128)} %bitcast.25, s32[32,128]{1,0:T(8,128)} %bitcast.24, f32[1,2048]{1,0:T(1,128)} %bitcast.20, bf16[4096,2048]{1,0:T(8,128)(2,1)} %feat_hbm.1), custom_call_target="tpu_custom_call" | custom-call | tf_op jit(solution)/shard_map/front/pallas_call | solution.py:162
  7.9 3.4 %collective-permute-start.2 = (f32[1,5120]{1,0:T(1,128)S(1)}, f32[1,5120]{1,0:T(1,128)S(1)}, u32[]{:S(2)}, u32[]{:S(2)}) collective-permute-start(f32[1,5120]{1,0:T(1,128)S(1)} %get-tuple-element.18.p0), channel_id=1, source_target_pairs={{0,3},{1,0},{2,1},{3,2},{4,7},{5,4},{6,5},{7,6},{8,11},{9,8},{10,9... | collective-permute-start | bytes 61448 | tf_op jit(solution)/shard_map/ppermute | solution.py:478
  11.3 0.5 collective-permute-start.1
  11.8 0.6 collective-permute-start
  12.4 0.0 copy-done
  12.4 0.0 copy-done.1
  12.4 2.5 %place.1 = (f32[4224,128]{1,0:T(8,128)S(1)}, f32[128,128]{1,0:T(8,128)S(1)}) custom-call(f32[8,1024]{1,0:T(8,128)S(1)} %get-tuple-element.20.route_ref.route_hbm, s32[1,4096]{1,0:T(1,128)S(1)} %bitcast.17, f32[1024,256]{1,0:T(8,128)S(1)} %copy-done), custom_call_target="tpu_custom_call" | custom-call | tf_op jit(solution)/shard_map/place/pallas_call | solution.py:212
  14.9 0.0 collective-permute-done.2.p3
  14.9 0.5 collective-permute-done.1.p2
  15.4 0.2 collective-permute-done.p1
  15.7 0.0 copy-done.4
  15.7 0.0 copy-start.2
  15.7 2.5 %grad.1 = (f32[32,16,128]{2,1,0:T(8,128)S(1)}, bf16[128,4096]{1,0:T(8,128)(2,1)S(1)}, bf16[128,4096]{1,0:T(8,128)(2,1)S(1)}) custom-call(f32[1,5120]{1,0:T(1,128)S(1)} %get-tuple-element.18.p0, f32[1,5120]{1,0:T(1,128)S(1)} %collective-permute-done.p1, f32[1,5120]{1,0:T(1,128)S(1)} %collective-permute-done.1.p2, f32[1,5120]{1,0:T(1,128)S(1)} %collective-permute-done.2.p3, ...), custom_call_target="tpu_custom_call" | custom-call | tf_op jit(solution)/shard_map/grad/pallas_call | solution.py:260
  18.2 18.6 %all_to_all.15.grads_ref = f32[32,16,128]{2,1,0:T(8,128)S(1)} all-to-all(f32[32,16,128]{2,1,0:T(8,128)S(1)} %get-tuple-element.22), channel_id=1, replica_groups=mesh['z'=4,'y'=4,'core'=2,'feat'=4] {'core','z','y'}, dimensions={0} | all-to-all | bytes 524288 | tf_op jit(solution)/shard_map/all_to_all | solution.py:483
  36.8 0.0 copy-done.2
  36.8 3.8 %new.1 = (f32[1,2048]{1,0:T(1,128)}, f32[4224,128]{1,0:T(8,128)S(1)}) custom-call(f32[32,16,128]{2,1,0:T(8,128)S(1)} %all_to_all.15.grads_ref, f32[1,2048]{1,0:T(1,128)S(1)} %bitcast.21, f32[128,128]{1,0:T(8,128)S(1)} %get-tuple-element.21.meta_ref, bf16[128,4096]{1,0:T(8,128)(2,1)S(1)} %get-tuple-element.23.owner_ref, ...), custom_call_target="tpu_custom_call", output_to_operand_aliasing={{1}: (6, {})} | custom-call | tf_op jit(solution)/shard_map/new/pallas_call | solution.py:312
  40.6 0.0 copy-start.3
  40.6 0.0 copy-start.5
  40.6 36.0 %all_to_all.16 = f32[128,1,4224]{2,1,0:T(1,128)S(1)} all-to-all(f32[128,1,4224]{2,1,0:T(1,128)S(1)} %bitcast.14), channel_id=1, replica_groups=mesh['z'=4,'y'=4,'core'=2,'feat'=4] {'z','y','core','feat'}, dimensions={0} | all-to-all | bytes 4325376 | tf_op jit(solution)/shard_map/all_to_all | solution.py:488
  76.7 0.0 copy-done.3
  76.7 0.0 copy-done.5
  76.7 4.4 %members.1 = (f32[32,256]{1,0:T(8,128)S(1)}, f32[128,128]{1,0:T(8,128)S(1)}, f32[8,1024]{1,0:T(8,128)S(1)}) custom-call(f32[4224,128]{1,0:T(8,128)S(1)} %bitcast.15, f32[32,256]{1,0:T(8,128)S(1)} %copy-done.3, s32[1,32]{1,0:T(1,128)S(1)} %bitcast.23, f32[8,1024]{1,0:T(8,128)S(1)} %get-tuple-element.20.route_ref.route_hbm), custom_call_target="tpu_custom_call" | custom-call | tf_op jit(solution)/shard_map/members/pallas_call | solution.py:431
  81.0 12.9 %all_to_all.17 = f32[128,1,128]{2,1,0:T(1,128)S(1)} all-to-all(f32[128,1,128]{2,1,0:T(1,128)S(1)} %bitcast.19), channel_id=1, replica_groups=mesh['z'=4,'y'=4,'core'=2,'feat'=4] {'core','z','y','feat'}, dimensions={0} | all-to-all | bytes 131072 | tf_op jit(solution)/shard_map/all_to_all | solution.py:488
  93.9 0.8 collect.1
Async XLA Ops:
  0.6 11.8 %copy-start = (f32[1024,256]{1,0:T(8,128)S(1)}, f32[1024,256]{1,0:T(8,128)}, u32[]{:S(2)}) copy-start(f32[1024,256]{1,0:T(8,128)} %rows_ref.1) | copy-start | bytes 3145732
  0.6 11.8 %copy-start.1 = (s32[4096]{0:T(1024)S(1)}, s32[4096]{0:T(1024)}, u32[]{:S(2)}) copy-start(s32[4096]{0:T(1024)} %param.12) | copy-start | bytes 49156
  0.7 15.0 %copy-start.4 = (f32[4096]{0:T(1024)S(1)}, f32[4096]{0:T(1024)}, u32[]{:S(2)}) copy-start(f32[4096]{0:T(1024)} %param.11) | copy-start | bytes 49156
  7.9 7.0 %collective-permute-start.2 = (f32[1,5120]{1,0:T(1,128)S(1)}, f32[1,5120]{1,0:T(1,128)S(1)}, u32[]{:S(2)}, u32[]{:S(2)}) collective-permute-start(f32[1,5120]{1,0:T(1,128)S(1)} %get-tuple-element.18.p0), channel_id=1, source_target_pairs={{0,3},{1,0},{2,1},{3,2},{4,7},{5,4},{6,5},{7,6},{8,11},{9,8},{10,9... | collective-permute-start | bytes 61448 | tf_op jit(solution)/shard_map/ppermute | solution.py:478
  11.3 4.1 %collective-permute-start.1 = (f32[1,5120]{1,0:T(1,128)S(1)}, f32[1,5120]{1,0:T(1,128)S(1)}, u32[]{:S(2)}, u32[]{:S(2)}) collective-permute-start(f32[1,5120]{1,0:T(1,128)S(1)} %get-tuple-element.18.p0), channel_id=1, source_target_pairs={{0,2},{1,3},{2,0},{3,1},{4,6},{5,7},{6,4},{7,5},{8,10},{9,11},{10,... | collective-permute-start | bytes 61448 | tf_op jit(solution)/shard_map/ppermute | solution.py:478
  11.8 3.8 %collective-permute-start = (f32[1,5120]{1,0:T(1,128)S(1)}, f32[1,5120]{1,0:T(1,128)S(1)}, u32[]{:S(2)}, u32[]{:S(2)}) collective-permute-start(f32[1,5120]{1,0:T(1,128)S(1)} %get-tuple-element.18.p0), channel_id=1, source_target_pairs={{0,1},{1,2},{2,3},{3,0},{4,5},{5,6},{6,7},{7,4},{8,9},{9,10},{10,1... | collective-permute-start | bytes 61448 | tf_op jit(solution)/shard_map/ppermute | solution.py:478
  15.7 21.1 %copy-start.2 = (f32[2048]{0:T(1024)S(1)}, f32[2048]{0:T(1024)}, u32[]{:S(2)}) copy-start(f32[2048]{0:T(1024)} %param.10) | copy-start | bytes 24580
  40.6 36.1 %copy-start.3 = (f32[32,256]{1,0:T(8,128)S(1)}, f32[32,256]{1,0:T(8,128)}, u32[]{:S(2)}) copy-start(f32[32,256]{1,0:T(8,128)} %params_ref.1) | copy-start | bytes 98308
  40.6 36.0 %copy-start.5 = (s32[32]{0:T(128)S(1)}, s32[32]{0:T(128)}, u32[]{:S(2)}) copy-start(s32[32]{0:T(128)} %param.15) | copy-start | bytes 388
